TPU v7x, 256 devices: a whole 4x4x8 slice. The times are simulated.
256 devices in a mesh: pairs: 64 (over y, z, core), dom: 4 (over x).
Axes of the slice: x: 4, y: 4, z: 8, core: 2. Of those that a mesh axis runs over, the one named last changes fastest.
Arguments:
- amplitude: bfloat16 [512, 384, 384], P('pairs', 'dom'), may hold values from -2 to 2
- integrals: bfloat16 [512, 384, 384], P('pairs', 'dom'), may hold values from -6 to 6
- virtual_energy: float32 [512, 384], P('pairs'), may hold values from 0.2 to 1.5
- occupied_gap: float32 [512], P('pairs'), may hold values from 0.3 to 1.5
- pair_slot: int32 [512], replicated, may hold values from 0 to 511, as said below
- coupling_source: int32 [8192], replicated, may hold values from 0 to 511, as said below
- coupling_target: int32 [8192], replicated, may hold values from 0 to 511, as said below
- coupling_fock: float32 [8192], P(('pairs', 'dom')), may hold values from -3 to 3
- coupling_intersection: bfloat16 [8192, 384, 384], P(('pairs', 'dom')), may hold values from -0.3125 to 0.3125
Outputs:
- updated_amplitude: float32 [512, 384, 384], P('pairs', 'dom')
- residual: float32 [512, 384, 384], P('pairs', 'dom')
Inputs may be any that keep to these rules, and one draw needn't show every extreme that they name: A permutation: pair p is stored at position pair_slot[p], which lies on index pair_slot[p] // 8 of pairs. `coupling_target`: coupling c is held by index c // 128 of pairs, and its target pair is stored on that same index; the two couplings that share a source pair on one holder have different targets. `coupling_source`: among the 128 couplings of one holder, every source pair appears in exactly two, and there are 64 distinct source pairs; of the pairs stored on any one index of pairs, a holder uses at most 2 distinct ones as sources, and exactly 2 for some indices on every holder.
All inputs are finite; a program needn't handle non-finite values.
Results may differ from a plain program's by a relative error of at most 0.0024.
Values may be sent and summed in bfloat16 or wider, within the bound.
No kernel may reach another device: no remote copies, remote signals or barrier semaphores. Data moves between devices by JAX's collectives and lax.ppermute only.
A program may use at most 128 MiB of HBM per device.

v0:
```python
import jax
import jax.numpy as jnp
from jax import lax
from jax.sharding import PartitionSpec as P

SRC_CAP = 2


def lookup(table, indices):
    places = jnp.arange(table.shape[0], dtype=jnp.int32)
    return jnp.sum(jnp.where(indices[:, None] == places[None, :], table[None, :], 0), axis=1)


def per_device(
    amplitude,
    integrals,
    virtual_energy,
    occupied_gap,
    pair_slot,
    coupling_source,
    coupling_target,
    coupling_fock,
    coupling_intersection,
):
    holders = lax.axis_size("pairs")
    quarters = lax.axis_size("dom")
    own_pair = lax.axis_index("pairs")
    own_quarter = lax.axis_index("dom")
    pair_count, row_count, width = amplitude.shape
    couplings = coupling_source.shape[0] // holders
    quarter_couplings = coupling_intersection.shape[0]
    source_slot = lookup(pair_slot, coupling_source).reshape(holders, couplings)
    target_slot = lookup(pair_slot, coupling_target).reshape(holders, couplings)
    source_owner = source_slot // pair_count
    source_local = source_slot % pair_count
    held_owner = lax.dynamic_index_in_dim(source_owner, own_pair, 0, keepdims=False)
    held_target = lax.dynamic_index_in_dim(target_slot, own_pair, 0, keepdims=False) % pair_count
    local_numbers = jnp.arange(pair_count, dtype=jnp.int32)
    capacity = 2 * SRC_CAP
    positions = jnp.arange(couplings, dtype=jnp.int32)
    earlier = positions[None, :] < positions[:, None]
    same = source_owner[:, :, None] == source_owner[:, None, :]
    rank = jnp.sum(same & earlier[None], axis=2)
    held_rank = lax.dynamic_index_in_dim(rank, own_pair, 0, keepdims=False)
    slot_numbers = jnp.arange(capacity, dtype=jnp.int32)
    chosen = (source_owner[:, None, :] == own_pair) & (
        rank[:, None, :] == slot_numbers[None, :, None]
    )
    picked = jnp.sum(jnp.where(chosen, source_local[:, None, :], 0), axis=2)
    held_slot = held_owner * capacity + held_rank
    energy_rows = lax.dynamic_slice_in_dim(virtual_energy, own_quarter * row_count, row_count, 1)
    denominator = energy_rows[:, :, None] + virtual_energy[:, None, :] + occupied_gap[:, None, None]
    target_select = (held_target[None, :] == local_numbers[:, None]).astype(jnp.bfloat16)
    quarter_select = lax.dynamic_slice_in_dim(
        target_select, own_quarter * quarter_couplings, quarter_couplings, 1
    )
    current = amplitude.astype(jnp.float32)
    sent = current.astype(jnp.bfloat16)
    outgoing = jnp.take(sent, picked.reshape(-1), axis=0).reshape(
        holders, capacity, row_count, width
    )
    arrived = lax.all_to_all(outgoing, "pairs", split_axis=0, concat_axis=0, tiled=True)
    held_rows = jnp.take(arrived.reshape(holders * capacity, row_count, width), held_slot, axis=0)
    grouped = held_rows.reshape(quarters, quarter_couplings, row_count, width)
    whole = lax.all_to_all(grouped, "dom", split_axis=0, concat_axis=2, tiled=True).reshape(
        quarter_couplings, quarters * row_count, width
    )
    left = jnp.einsum(
        "cab,cbd->cad", coupling_intersection, whole, preferred_element_type=jnp.float32
    ).astype(jnp.bfloat16)
    projected = jnp.einsum(
        "cad,ced->cae", left, coupling_intersection, preferred_element_type=jnp.float32
    )
    coupled_term = (coupling_fock[:, None, None] * projected).astype(jnp.bfloat16)
    partial_sum = jnp.dot(
        quarter_select,
        coupled_term.reshape(quarter_couplings, -1),
        preferred_element_type=jnp.float32,
    )
    partial_sum = partial_sum.reshape(pair_count, quarters * row_count, width)
    coupled = lax.psum_scatter(partial_sum, "dom", scatter_dimension=1, tiled=True)
    residual = integrals.astype(jnp.float32) + denominator * current - coupled
    current = current - residual / denominator
    return (current, residual)


def solution(mesh):
    in_specs = (
        P("pairs", "dom", None),
        P("pairs", "dom", None),
        P("pairs", None),
        P("pairs"),
        P(),
        P(),
        P(),
        P(("pairs", "dom")),
        P(("pairs", "dom"), None, None),
    )
    out_specs = (P("pairs", "dom", None), P("pairs", "dom", None))
    return jax.shard_map(
        per_device, mesh=mesh, in_specs=in_specs, out_specs=out_specs, check_vma=False
    )
```

profile of v0, /device:TPU:2, one launch (start us, length us, event | category | flops | bytes accessed | tf_op | source)
XLA Modules:
  0.0 700.1 jit_solution(15263810342996406017)
XLA Ops:
  7.2 7.3 %select_reduce_fusion.1 = (s32[8192]{0:T(1024)S(1)}, s32[8192]{0:T(1024)S(1)}) fusion(s32[512]{0:T(512)} %param.13, s32[8192]{0:T(1024)} %param.15, s32[8192]{0:T(1024)} %param.14), kind=kLoop, calls=%fused_computation.6 | loop fusion | flops 25149440 | bytes 133120 | tf_op jit(solution)/shard_map/reduce_sum | solution.py:11
  14.5 2.6 convert_reduce_fusion
  17.1 0.1 select_reduce_fusion.2
  17.3 0.1 copy.36
  17.4 0.1 copy.35
  17.5 0.1 reshape.220
  17.6 11.8 %gather_fusion = bf16[256,96,384]{2,1,0:T(8,128)(2,1)} fusion(bf16[8,96,384]{2,1,0:T(8,128)(2,1)} %param.9, s32[1024]{0:T(1024)S(1)} %pad_clamp_fusion.1), kind=kCustom, calls=%fused_computation | custom fusion | bytes 37749760 | tf_op jit(solution)/shard_map/jit(_take)/gather | solution.py:59
  29.4 13.9 %broadcast_select_fusion = bf16[64,4,96,384]{3,2,1,0:T(8,128)(2,1)} fusion(bf16[64,4,96,384]{3,2,1,0:T(8,128)(2,1)} %bitcast.60, pred[64,4]{1,0:T(8,128)(4,1)S(1)} %copy.35), kind=kLoop, calls=%fused_computation.3 | loop fusion | flops 9437184 | bytes 37748992 | tf_op jit(solution)/shard_map/jit(_take)/select_n | solution.py:59
  43.2 12.5 %all-to-all-start = ((bf16[64,4,96,384]{3,2,1,0:T(8,128)(2,1)}), bf16[64,4,96,384]{3,2,1,0:T(8,128)(2,1)}, u32[]{:S(2)}, u32[]{:S(2)}) async-start(bf16[64,4,96,384]{3,2,1,0:T(8,128)(2,1)} %broadcast_select_fusion), calls=%async_computation | async-start | bytes 37748736 | tf_op jit(solution)/shard_map/all_to_all | solution.py:62
  55.7 0.5 broadcast.219
  56.2 0.7 fusion.24
  56.9 0.1 add.141
  57.0 408.7 %all-to-all-done = bf16[64,4,96,384]{3,2,1,0:T(8,128)(2,1)} async-done(((bf16[64,4,96,384]{3,2,1,0:T(8,128)(2,1)}), bf16[64,4,96,384]{3,2,1,0:T(8,128)(2,1)}, u32[]{:S(2)}, u32[]{:S(2)}) %all-to-all-start) | async-done | bytes 18874400 | tf_op jit(solution)/shard_map/all_to_all | solution.py:62
  465.7 14.0 %gather_fusion.1 = bf16[128,96,384]{2,1,0:T(8,128)(2,1)} fusion(bf16[256,96,384]{2,1,0:T(8,128)(2,1)} %bitcast.6, s32[1024]{0:T(1024)S(1)} %pad_clamp_fusion), kind=kCustom, calls=%fused_computation.1 | custom fusion | bytes 18874880 | tf_op jit(solution)/shard_map/jit(_take)/gather | solution.py:63
  479.7 8.6 %broadcast_select_fusion.1 = bf16[4,32,96,384]{3,2,1,0:T(8,128)(2,1)} fusion(bf16[4,32,96,384]{3,2,1,0:T(8,128)(2,1)} %bitcast.61, pred[4,32]{1,0:T(4,128)(4,1)S(1)} %compare_and_fusion.1), kind=kLoop, calls=%fused_computation.13 | loop fusion | flops 4718592 | bytes 18874496 | tf_op jit(solution)/shard_map/jit(_take)/select_n | solution.py:63
  488.3 6.3 all-to-all-start.1
  494.6 0.0 reduce-scatter.2.cloned.1.call-start
  494.6 104.5 %all-to-all-done.1 = bf16[4,32,96,384]{3,2,1,0:T(8,128)(2,1)} async-done(((bf16[4,32,96,384]{3,2,1,0:T(8,128)(2,1)}), bf16[4,32,96,384]{3,2,1,0:T(8,128)(2,1)}, u32[]{:S(2)}, u32[]{:S(2)}) %all-to-all-start.1) | async-done | bytes 9437216 | tf_op jit(solution)/shard_map/all_to_all | solution.py:65
  599.1 0.0 copy-start.4
  599.1 9.2 %copy.37 = bf16[1,32,4,96,384]{4,3,2,1,0:T(8,128)(2,1)} copy(bf16[1,32,4,96,384]{4,3,1,2,0:T(8,128)(2,1)} %bitcast.11) | data formatting | bytes 18874368 | tf_op jit(solution)/shard_map/all_to_all | solution.py:65
  608.3 0.0 copy-done.4
  608.3 20.8 %multiply_convert_fusion = bf16[32,384,384]{2,1,0:T(8,128)(2,1)} fusion(f32[32]{0:T(128)S(1)} %copy-done.4, bf16[32,384,384]{2,1,0:T(8,128)(2,1)} %param.17, bf16[32,384,384]{2,1,0:T(8,128)(2,1)} %bitcast.63), kind=kOutput, calls=%fused_computation.2 | convolution fusion | flops 7261913088 | bytes 28311680 | tf_op jit(solution)/shard_map/cad,ced->cae/dot_general | solution.py:71
  629.1 0.0 copy-start.2
  629.1 0.0 copy-start
  629.1 0.0 copy-start.1
  629.1 0.0 copy-start.3
  629.2 11.2 %fusion = f32[8,384,384]{2,0,1:T(8,128)} fusion(pred[8,128]{1,0:T(8,128)(4,1)S(1)} %iota_compare_fusion.4, s32[]{:T(128)S(6)} %select_n.105, bf16[4,8,384,384]{3,2,1,0:T(8,128)(2,1)} %bitcast.62), kind=kOutput, calls=%fused_computation.8 | convolution fusion | flops 75497472 | bytes 14156804 | tf_op jit(solution)/shard_map/dot_general | solution.py:75
  640.4 0.0 reduce-scatter.2.cloned.1.call-update
  640.4 0.0 copy-done.2
  640.4 0.1 constant_dynamic-slice_fusion.3
  640.5 0.1 copy.34
  640.6 48.4 %reduce-scatter.2.cloned.1.call-done = f32[8,96,384]{2,0,1:T(8,128)} async-done(((f32[8,384,384]{2,0,1:T(8,128)}), f32[8,96,384]{2,0,1:T(8,128)}) %reduce-scatter.2.cloned.1.call-update) | async-done | bytes 1179664 | tf_op jit(solution)/shard_map/reduce_scatter | solution.py:81
  689.0 0.0 copy-done
  689.0 0.0 copy-done.1
  689.0 0.0 copy-done.3
  689.0 1.8 convert_subtract_fusion
  690.8 1.2 copy.41
  692.0 1.2 copy.42
  (11 shorter events, 0.1 us)
Async XLA Ops:
  43.2 422.4 %all-to-all-start = ((bf16[64,4,96,384]{3,2,1,0:T(8,128)(2,1)}), bf16[64,4,96,384]{3,2,1,0:T(8,128)(2,1)}, u32[]{:S(2)}, u32[]{:S(2)}) async-start(bf16[64,4,96,384]{3,2,1,0:T(8,128)(2,1)} %broadcast_select_fusion), calls=%async_computation | async-start | bytes 37748736 | tf_op jit(solution)/shard_map/all_to_all | solution.py:62
  488.3 110.9 %all-to-all-start.1 = ((bf16[4,32,96,384]{3,2,1,0:T(8,128)(2,1)}), bf16[4,32,96,384]{3,2,1,0:T(8,128)(2,1)}, u32[]{:S(2)}, u32[]{:S(2)}) async-start(bf16[4,32,96,384]{3,2,1,0:T(8,128)(2,1)} %broadcast_select_fusion.1), calls=%async_computation.1 | async-start | bytes 18874368 | tf_op jit(solution)/shard_map/all_to_all | solution.py:65
  494.6 194.4 %reduce-scatter.2.cloned.1.call-start = ((), (), s32[]{:S(2)}) async-start(), calls=%async_computation.3 | async-start | bytes 5898240 | tf_op jit(solution)/shard_map/reduce_scatter | solution.py:81
  599.1 9.2 %copy-start.4 = (f32[32]{0:T(128)S(1)}, f32[32]{0:T(128)}, u32[]{:S(2)}) copy-start(f32[32]{0:T(128)} %param.16) | copy-start | bytes 388
  629.1 11.3 %copy-start.2 = (f32[8,384]{1,0:T(8,128)S(1)}, f32[8,384]{1,0:T(8,128)}, u32[]{:S(2)}) copy-start(f32[8,384]{1,0:T(8,128)} %param.11) | copy-start | bytes 36868
  629.1 59.8 %copy-start = (bf16[8,96,384]{2,1,0:T(8,128)(2,1)S(1)}, bf16[8,96,384]{2,1,0:T(8,128)(2,1)}, u32[]{:S(2)}) copy-start(bf16[8,96,384]{2,1,0:T(8,128)(2,1)} %param.9) | copy-start | bytes 1769476
  629.1 59.8 %copy-start.1 = (bf16[8,96,384]{2,1,0:T(8,128)(2,1)S(1)}, bf16[8,96,384]{2,1,0:T(8,128)(2,1)}, u32[]{:S(2)}) copy-start(bf16[8,96,384]{2,1,0:T(8,128)(2,1)} %param.10) | copy-start | bytes 1769476
  629.1 59.8 %copy-start.3 = (f32[8]{0:T(128)S(1)}, f32[8]{0:T(128)}, u32[]{:S(2)}) copy-start(f32[8]{0:T(128)} %param.12) | copy-start | bytes 100
Sparse Core Ops, SparseCore 0:
  640.5 48.3 reduce-scatter.1
where the time goes:
time: 703 us; the launch traced here: 700 us
  waiting for transfers between devices  562 us (80%)
  local copies, waits for them, and re-layouts  38.5 us (5%)
  other arithmetic  35 us (5%)
  matrix products  32 us (5%)
  starting transfers between devices  18.8 us (3%)
  between operations  14.1 us (2%)
    all_to_all x1, waiting for transfers between devices, per_device(): lax.all_to_all(outgoing, 'pairs', split_axis=0, concat_axis=0, tiled=True)  409 us
    all_to_all x1, waiting for transfers between devices, per_device(): lax.all_to_all(grouped, 'dom', split_axis=0, concat_axis=2, tiled=True)  105 us
    reduce_scatter x1, waiting for transfers between devices, per_device(): lax.psum_scatter(partial_sum, 'dom', scatter_dimension=1, tiled=True)  48.4 us
    dot_general x1, matrix products, per_device(): jnp.einsum('cad,ced->cae', left, coupling_intersection, preferred_element...  20.8 us
  transfers between devices with their start and end apart: 3, of which 3 were waited for; matrix products, arithmetic and copies ran while one was open for 0% of the time, Pallas kernels for 0%

commit v1 on v0

v1 whole, which is shorter than its diff:
```python
import jax
import jax.numpy as jnp
from jax import lax
from jax.experimental import pallas as pl
from jax.experimental.pallas import tpu as pltpu
from jax.sharding import Mesh, PartitionSpec as P

COLUMNS = 128
SPLITS = 2
GROUPS = (
    ("ring", ((0, 0),)),
    ("gather", ((0, 1), (1, 0), (1, 1), (2, 0), (2, 1))),
)
STAGES = ((0, 1), (2,))
UNROLL = 4
RING_PLACE = (0, 2, 4, 6, 7, 5, 3, 1)
STAGE_FLOPS = 12_000_000_000
STAGE_BYTES = 36_000_000


def lookup(table, indices):
    places = jnp.arange(table.shape[0], dtype=jnp.int32)
    return jnp.sum(jnp.where(indices[..., None] == places, table, 0), axis=-1)


def ring_gather(block):
    count = lax.axis_size("z")
    up = [(i, (i + 1) % count) for i in range(count)]
    down = [(i, (i - 1) % count) for i in range(count)]
    parts = [block]
    above = below = block
    for _ in range(count // 2 - 1):
        above = lax.ppermute(above, "z", up)
        below = lax.ppermute(below, "z", down)
        parts += [above, below]
    half = block.shape[1] // 2
    above = lax.ppermute(above[:, :half], "z", up)
    below = lax.ppermute(below[:, half:], "z", down)
    parts.append(jnp.concatenate([above, below], axis=1))
    return jnp.stack(parts)


def split(amplitude, piece):
    pairs, _, _ = amplitude.shape

    def kernel(in_ref, *out_refs):
        for out_ref, (_, members) in zip(out_refs, GROUPS):
            for n, (j, r) in enumerate(members):
                rows = slice(r * piece, (r + 1) * piece)
                lanes = slice(j * COLUMNS, (j + 1) * COLUMNS)
                for p in range(pairs):
                    out_ref[n, p] = in_ref[p, rows, lanes]

    return pl.pallas_call(
        kernel,
        out_shape=[
            jax.ShapeDtypeStruct((len(members), pairs, piece, COLUMNS), amplitude.dtype)
            for _, members in GROUPS
        ],
        name="split",
    )(amplitude)


def pick(arrays, member, index, outputs, name, cost=None):
    piece, lanes = arrays[0].shape[-2:]
    count = index.shape[0] // outputs
    sizes = [array.shape[0] * array.shape[2] for array in arrays]

    def kernel(index_ref, *refs):
        in_refs = refs[: len(arrays)]
        out_refs = refs[len(arrays) : len(arrays) + outputs]
        held, sems = refs[-2:]
        copies = []
        start = 0
        for n, ref in enumerate(in_refs):
            for lead in range(arrays[n].shape[0]):
                size = arrays[n].shape[2]
                copy = pltpu.make_async_copy(
                    ref.at[lead, member], held.at[pl.ds(start, size)], sems.at[len(copies)]
                )
                copy.start()
                copies.append(copy)
                start += size
        for copy in copies:
            copy.wait()

        def body(i, carry):
            for n in range(outputs):
                out_refs[n][i] = held[index_ref[n * count + i]]
            return carry

        lax.fori_loop(0, count, body, 0, unroll=8)

    result = pl.pallas_call(
        kernel,
        in_specs=[pl.BlockSpec(memory_space=pltpu.SMEM)] + [pl.BlockSpec(memory_space=pltpu.HBM if array.shape[1] > 1 else pl.ANY) for array in arrays],
        out_specs=[pl.BlockSpec(memory_space=pltpu.VMEM)] * outputs,
        out_shape=[jax.ShapeDtypeStruct((count, piece, lanes), arrays[0].dtype)] * outputs,
        scratch_shapes=[
            pltpu.VMEM((sum(sizes), piece, lanes), arrays[0].dtype),
            pltpu.SemaphoreType.DMA((sum(array.shape[0] for array in arrays),)),
        ],
        compiler_params=pltpu.CompilerParams(vmem_limit_bytes=60 * 1024 * 1024),
        cost_estimate=cost,
        name=name,
    )(index, *arrays)
    return result


def make_couple(stage, first, final, count, rows, width, pairs, quarters):
    columns = len(stage) * COLUMNS
    begin = stage[0] * COLUMNS
    blocks = len(stage) * SPLITS
    piece = rows // SPLITS

    def kernel(target, fock, s_ref, *rest):
        rest = list(rest)
        amp_refs = [rest.pop(0) for _ in range(blocks)]
        base_ref = None if first else rest.pop(0)
        out_ref = rest.pop(0)
        acc = rest.pop(0) if final else out_ref
        step = pl.program_id(0)

        @pl.when(step == 0)
        def _():
            for p in range(pairs):
                if first:
                    acc[p] = jnp.zeros((width, width), jnp.float32)
                else:
                    acc[p] = base_ref[p]

        lefts = []
        for g in range(UNROLL):
            strips = []
            for b in range(0, blocks, SPLITS):
                pieces = [amp_refs[b + r][q, g] for q in range(quarters) for r in range(SPLITS)]
                strips.append(jnp.concatenate(pieces, axis=0))
            amp = strips[0] if len(strips) == 1 else jnp.concatenate(strips, axis=1)
            left = jnp.dot(s_ref[g], amp, preferred_element_type=jnp.float32)
            lefts.append(left.astype(jnp.bfloat16))
        for g in range(UNROLL):
            part = lax.dot_general(
                lefts[g],
                s_ref[g, :, begin : begin + columns],
                (((1,), (1,)), ((), ())),
                preferred_element_type=jnp.float32,
            )
            c = step * UNROLL + g
            acc[target[c]] += fock[c] * part
        if final:

            @pl.when(step == count // UNROLL - 1)
            def _():
                for p in range(pairs):
                    for q in range(quarters):
                        out_ref[q, p] = acc[p, q * rows : (q + 1) * rows, :].astype(jnp.bfloat16)

    whole = pl.BlockSpec((pairs, width, width), lambda i, *_: (0, 0, 0), pipeline_mode=pl.Buffered(1))
    in_specs = [pl.BlockSpec((UNROLL, width, width), lambda i, *_: (i, 0, 0))]
    in_specs += [pl.BlockSpec((quarters, UNROLL, piece, COLUMNS), lambda i, *_: (0, i, 0, 0))] * blocks
    if not first:
        in_specs.append(whole)
    scratch = []
    if final:
        out_shape = jax.ShapeDtypeStruct((quarters, pairs, rows, width), jnp.bfloat16)
        out_specs = pl.BlockSpec((quarters, pairs, rows, width), lambda i, *_: (0, 0, 0, 0))
        scratch.append(pltpu.VMEM((pairs, width, width), jnp.float32))
    else:
        out_shape = jax.ShapeDtypeStruct((pairs, width, width), jnp.float32)
        out_specs = whole
    return pl.pallas_call(
        kernel,
        grid_spec=pltpu.PrefetchScalarGridSpec(
            num_scalar_prefetch=2,
            grid=(count // UNROLL,),
            in_specs=in_specs,
            out_specs=out_specs,
            scratch_shapes=scratch,
        ),
        out_shape=out_shape,
        compiler_params=pltpu.CompilerParams(vmem_limit_bytes=60 * 1024 * 1024),
        cost_estimate=pl.CostEstimate(
            flops=8 * count * width * width * columns,
            bytes_accessed=count * width * width * 3,
            transcendentals=0,
        ),
        name="couple",
    )


def per_device(
    amplitude,
    integrals,
    virtual_energy,
    occupied_gap,
    pair_slot,
    coupling_source,
    coupling_target,
    coupling_fock,
    coupling_intersection,
):
    ny, nz, nc, quarters = (lax.axis_size(a) for a in ("y", "z", "core", "dom"))
    y, z, core, me = (lax.axis_index(a) for a in ("y", "z", "core", "dom"))
    pairs, rows, width = amplitude.shape
    piece = rows // SPLITS
    holders = ny * nz * nc
    held = coupling_source.shape[0] // holders
    count = coupling_intersection.shape[0]
    capacity = nz * nc * 2

    with jax.named_scope("tables"):
        sources = coupling_source.reshape(ny, nz, nc, held)
        sources = lax.dynamic_index_in_dim(sources, z, 1, keepdims=False)
        sources = lax.dynamic_index_in_dim(sources, core, 1, keepdims=False)
        slots = lookup(pair_slot, sources)
        local = slots % pairs
        owner = slots // pairs
        mine = y * (nz * nc) + jnp.arange(nz * nc, dtype=jnp.int32)
        match = owner[:, None, :] == mine[None, :, None]
        low = jnp.min(jnp.where(match, local[:, None, :], pairs - 1), axis=2)
        high = jnp.max(jnp.where(match, local[:, None, :], 0), axis=2)
        picked = jnp.roll(jnp.stack([low, high], axis=2), -y, axis=0).reshape(ny, nz, nc, 2)
        z_numbers = jnp.arange(nz, dtype=jnp.int32)
        c_numbers = jnp.arange(nc, dtype=jnp.int32)
        ring_place = lookup(jnp.array(RING_PLACE, jnp.int32), (z_numbers - z) % nz)
        own_base = ((c_numbers != core) * (nz * pairs))[None, :] + (ring_place * pairs)[:, None]
        all_base = (z_numbers[:, None] * nc + c_numbers[None, :]) * pairs
        own_index = (picked + own_base[None, :, :, None]).reshape(-1)
        all_index = (picked + all_base[None, :, :, None]).reshape(-1)
        own_local = lax.dynamic_index_in_dim(local, y, 0, keepdims=False)
        own_owner = lax.dynamic_index_in_dim(owner, y, 0, keepdims=False)
        same = own_owner[:, None] == own_owner[None, :]
        least = jnp.min(jnp.where(same, own_local[None, :], pairs - 1), axis=1)
        second = (own_local > least).astype(jnp.int32)
        turned = (own_owner // (nz * nc) - y) % ny
        slot = turned * capacity + own_owner % (nz * nc) * 2 + second
        target = lax.dynamic_slice_in_dim(
            coupling_target, ((y * nz + z) * nc + core) * held + me * count, count, 0
        )
        target = lookup(pair_slot, target) % pairs

    def shift(array, step):
        return lax.ppermute(array, "y", [(i, (i + step) % ny) for i in range(ny)])

    stage_cost = pl.CostEstimate(flops=STAGE_FLOPS, bytes_accessed=STAGE_BYTES, transcendentals=0)
    landed = {}
    blocks = split(amplitude, piece)
    for (kind, members), block in zip(GROUPS, blocks):
        with jax.named_scope("along_z"):
            if kind == "ring":
                own = ring_gather(block)
                other = lax.ppermute(own, "core", [(i, 1 - i) for i in range(nc)])
                around, index = [own, other], own_index
            else:
                around, index = [lax.all_gather(block, ("z", "core"), axis=0)], all_index
        for n, member in enumerate(members):
            with jax.named_scope("along_y"):
                stay, ahead, far, back = pick(around, n, index, ny, "pick_y")
                from_back = shift(ahead, 1)
                from_ahead = shift(back, -1)
                from_far = shift(far, 2)
            with jax.named_scope("along_x"):
                here = [part[None, None] for part in (stay, from_ahead, from_far, from_back)]
                leaving = pick(here, 0, slot, 1, "pick_x", stage_cost)[0]
                arrived = lax.all_to_all(leaving, "dom", 0, 0, tiled=True)
            landed[member] = arrived.reshape(quarters, count, piece, COLUMNS)
    total = None
    for stage in STAGES:
        final = stage is STAGES[-1]
        couple = make_couple(stage, total is None, final, count, rows, width, pairs, quarters)
        args = [target, coupling_fock, coupling_intersection]
        args += [landed[j, r] for j in stage for r in range(SPLITS)]
        if total is not None:
            args.append(total)
        with jax.named_scope("couple"):
            total = couple(*args)
    with jax.named_scope("sum_x"):
        shares = lax.all_to_all(total, "dom", 0, 0, tiled=True)
    coupled = jnp.sum(shares.astype(jnp.float32), axis=0)
    energy_rows = lax.dynamic_slice_in_dim(virtual_energy, me * rows, rows, 1)
    denominator = energy_rows[:, :, None] + virtual_energy[:, None, :] + occupied_gap[:, None, None]
    current = amplitude.astype(jnp.float32)
    residual = integrals.astype(jnp.float32) + denominator * current - coupled
    return current - residual / denominator, residual


def solution(mesh):
    fine = Mesh(mesh.devices.reshape(4, 8, 2, 4), ("y", "z", "core", "dom"))
    chips = ("y", "z", "core")
    in_specs = (
        P(chips, "dom", None),
        P(chips, "dom", None),
        P(chips, None),
        P(chips),
        P(),
        P(),
        P(),
        P(chips + ("dom",)),
        P(chips + ("dom",), None, None),
    )
    out_specs = (P(chips, "dom", None), P(chips, "dom", None))
    return jax.shard_map(per_device, mesh=fine, in_specs=in_specs, out_specs=out_specs, check_vma=False)
```

time: 703 us -> 270 us (0.38)
  waiting for transfers between devices: 562 us -> 86.9 us
  Pallas kernels: 0 us -> 72 us
  starting transfers between devices: 18.8 us -> 76.7 us
  matrix products: 32 us -> 0 us
  other arithmetic: 35 us -> 6.55 us
  local copies, waits for them, and re-layouts: 38.5 us -> 11.7 us
    all_to_all x2 -> x7, waiting for transfers between devices: 513 us -> 55.1 us  [the longest x6 33 us: per_device(): arrived = lax.all_to_all(leaving, 'dom', 0, 0, tiled=True)]
    pallas_call x0 -> x15, Pallas kernels: none -> 72 us  [the longest x12 42 us: pick(): pl.pallas_call(kernel, in_specs=[pl.BlockSpec(memory_space=pltpu.SMEM)] +...]
    reduce_scatter x1 -> x0, waiting for transfers between devices: 48.4 us -> none  [per_device(): lax.psum_scatter(partial_sum, 'dom', scatter_dimension=1, tiled=True)]
    ppermute x0 -> x27, starting transfers between devices: none -> 41.9 us  [the longest x18 25.5 us: shift(): return lax.ppermute(array, 'y', [(i, (i + step) % ny) for i in range(ny)])]
    dot_general x2 -> x0, matrix products: 32 us -> none  [the longest x1 20.8 us: per_device(): jnp.einsum('cad,ced->cae', left, coupling_intersection, preferred_element...]
    gather x2 -> x0, local copies, waits for them, and re-layouts: 25.8 us -> none  [the longest x1 14 us: per_device(): jnp.take(arrived.reshape(holders * capacity, row_count, width), held_slot...]
    select_n x5 -> x3, other arithmetic: 22.5 us -> 0.55 us  [the longest x1 0.53 us: per_device(): target = lookup(pair_slot, target) % pairs]
    ppermute x0 -> x27, waiting for transfers between devices: none -> 17.8 us  [the longest x3 4.25 us: ring_gather(): below = lax.ppermute(below, 'z', down)]
  transfers between devices with their start and end apart: 3 -> 35, of which waited for: 3 -> 13; matrix products, arithmetic and copies ran while one was open for 0% -> 3% of each run, Pallas kernels for 0% -> 21%
where the time goes in v1:
time: 270 us; the launch traced here: 268 us
  waiting for transfers between devices  86.9 us (32%)
  starting transfers between devices  76.7 us (28%)
  Pallas kernels  72 us (27%)
  between operations  14.4 us (5%)
  local copies, waits for them, and re-layouts  11.7 us (4%)
  other arithmetic  6.55 us (2%)
    pallas_call x12, Pallas kernels, pick(): pl.pallas_call(kernel, in_specs=[pl.BlockSpec(memory_space=pltpu.SMEM)] +...  42 us
    all_to_all x6, waiting for transfers between devices, per_device(): arrived = lax.all_to_all(leaving, 'dom', 0, 0, tiled=True)  33 us
    all_to_all x6, starting transfers between devices, per_device(): arrived = lax.all_to_all(leaving, 'dom', 0, 0, tiled=True)  29.8 us
    pallas_call x2, Pallas kernels, per_device(): total = couple(*args)  28.1 us
    ppermute x18, starting transfers between devices, shift(): return lax.ppermute(array, 'y', [(i, (i + step) % ny) for i in range(ny)])  25.5 us
    all_to_all x1, waiting for transfers between devices, per_device(): shares = lax.all_to_all(total, 'dom', 0, 0, tiled=True)  22.1 us
    all_gather x1, waiting for transfers between devices, per_device(): around, index = ([lax.all_gather(block, ('z', 'core'), axis=0)], all_index)  14 us
    ppermute x3, starting transfers between devices, ring_gather(): below = lax.ppermute(below, 'z', down)  10.5 us
  transfers between devices with their start and end apart: 35, of which 13 were waited for; matrix products, arithmetic and copies ran while one was open for 3% of the time, Pallas kernels for 21%

profile of v1, /device:TPU:2, one launch (start us, length us, event | category | flops | bytes accessed | tf_op | source)
XLA Modules:
  0.0 268.3 jit_solution(8333659762068764044)
XLA Ops:
  7.2 2.0 split.1
  9.3 2.0 collective-permute-start.6
  11.3 4.0 %collective-permute-start.7 = (bf16[1,8,48,128]{3,2,1,0:T(8,128)(2,1)}, bf16[1,8,48,128]{3,2,1,0:T(8,128)(2,1)S(1)}, u32[]{:S(2)}, u32[]{:S(2)}) collective-permute-start(bf16[1,8,48,128]{3,2,1,0:T(8,128)(2,1)} %get-tuple-element.37), channel_id=1, source_target_pairs={{0,56},{8,0},{16,8},{24,16},{32,24},{40,32},{48,40},{56,48},{1,57}... | collective-permute-start | bytes 294920 | tf_op jit(solution)/shard_map/along_z/ppermute | solution.py:34
  15.3 0.8 select_reduce_fusion.3
  16.2 1.0 select_reduce_fusion
  17.5 0.9 bitcast_dynamic-update-slice_fusion.6
  18.5 3.2 %collective-permute-start.9 = (bf16[1,8,48,128]{3,2,1,0:T(8,128)(2,1)S(1)}, bf16[1,8,48,128]{3,2,1,0:T(8,128)(2,1)S(1)}, u32[]{:S(2)}, u32[]{:S(2)}) collective-permute-start(bf16[1,8,48,128]{3,2,1,0:T(8,128)(2,1)S(1)} %collective-permute-done.7), channel_id=1, source_target_pairs={{0,56},{8,0},{16,8},{24,16},{32,24},{40,32},{48,40},{56,48},{1,57}... | collective-permute-start | bytes 294920 | tf_op jit(solution)/shard_map/along_z/ppermute | solution.py:34
  21.8 2.5 collective-permute-done.8
  24.3 3.2 %collective-permute-start.11 = (bf16[1,8,48,128]{3,2,1,0:T(8,128)(2,1)S(1)}, bf16[1,8,48,128]{3,2,1,0:T(8,128)(2,1)S(1)}, u32[]{:S(2)}, u32[]{:S(2)}) collective-permute-start(bf16[1,8,48,128]{3,2,1,0:T(8,128)(2,1)S(1)} %collective-permute-done.9), channel_id=1, source_target_pairs={{0,56},{8,0},{16,8},{24,16},{32,24},{40,32},{48,40},{56,48},{1,57}... | collective-permute-start | bytes 294920 | tf_op jit(solution)/shard_map/along_z/ppermute | solution.py:34
  27.6 4.2 %collective-permute-done.11 = bf16[1,8,48,128]{3,2,1,0:T(8,128)(2,1)S(1)} collective-permute-done((bf16[1,8,48,128]{3,2,1,0:T(8,128)(2,1)S(1)}, bf16[1,8,48,128]{3,2,1,0:T(8,128)(2,1)S(1)}, u32[]{:S(2)}, u32[]{:S(2)}) %collective-permute-start.11) | collective-permute-done | bytes 98336 | tf_op jit(solution)/shard_map/along_z/ppermute | solution.py:34
  31.8 3.7 %collective-permute-start.13 = (bf16[1,4,48,128]{3,2,1,0:T(8,128)(2,1)S(1)}, bf16[1,4,48,128]{3,2,1,0:T(8,128)(2,1)S(1)}, u32[]{:S(2)}, u32[]{:S(2)}) collective-permute-start(bf16[1,4,48,128]{3,2,1,0:T(8,128)(2,1)S(1)} %slice.9), channel_id=1, source_target_pairs={{0,56},{8,0},{16,8},{24,16},{32,24},{40,32},{48,40},{56,48},{1,57}... | collective-permute-start | bytes 147464 | tf_op jit(solution)/shard_map/along_z/ppermute | solution.py:38
  35.7 2.5 collective-permute-done.13
  38.2 3.8 %collective-permute-done.12 = bf16[1,4,48,128]{3,2,1,0:T(8,128)(2,1)S(1)} collective-permute-done((bf16[1,4,48,128]{3,2,1,0:T(8,128)(2,1)S(1)}, bf16[1,4,48,128]{3,2,1,0:T(8,128)(2,1)S(1)}, u32[]{:S(2)}, u32[]{:S(2)}) %collective-permute-start.12) | collective-permute-done | bytes 49184 | tf_op jit(solution)/shard_map/along_z/ppermute | solution.py:37
  43.5 0.9 collective-permute-done.14.refs_1_
  44.3 0.9 copy-done.10
  45.2 3.6 %pick_y.8 = (bf16[32,48,128]{2,1,0:T(8,128)(2,1)}, bf16[32,48,128]{2,1,0:T(8,128)(2,1)}, bf16[32,48,128]{2,1,0:T(8,128)(2,1)}, bf16[32,48,128]{2,1,0:T(8,128)(2,1)}) custom-call(s32[128]{0:T(128)} %get-tuple-element.60.index_ref, bf16[8,1,8,48,128]{4,3,2,1,0:T(8,128)(2,1)} %copy-done.9, bf16[8,1,8,48,128]{4,3,2,1,0:T(8,128)(2,1)} %copy-done.10), custom_call_target="tpu_custom_call" | custom-call | tf_op jit(solution)/shard_map/along_y/pick_y/pallas_call | solution.py:94
  48.8 3.3 %collective-permute-start.15 = (bf16[32,48,128]{2,1,0:T(8,128)(2,1)}, bf16[32,48,128]{2,1,0:T(8,128)(2,1)S(1)}, u32[]{:S(2)}, u32[]{:S(2)}) collective-permute-start(bf16[32,48,128]{2,1,0:T(8,128)(2,1)} %get-tuple-element.39), channel_id=1, source_target_pairs={{0,192},{64,0},{128,64},{192,128},{1,193},{65,1},{129,65},{193,129... | collective-permute-start | bytes 1179656 | tf_op jit(solution)/shard_map/along_y/ppermute | solution.py:243
  52.6 1.0 collective-permute-start.17
  54.4 14.0 %all-gather.3.cloned.1.call-done = bf16[80,8,48,128]{3,2,1,0:T(8,128)(2,1)} async-done(((bf16[5,8,48,128]{3,2,1,0:T(8,128)(2,1)}), bf16[80,8,48,128]{3,2,1,0:T(8,128)(2,1)}) %all-gather.3.cloned.1.call-update) | async-done | bytes 7864336 | tf_op jit(solution)/shard_map/along_z/all_gather | solution.py:255
  68.4 3.6 %pick_y.6 = (bf16[32,48,128]{2,1,0:T(8,128)(2,1)}, bf16[32,48,128]{2,1,0:T(8,128)(2,1)}, bf16[32,48,128]{2,1,0:T(8,128)(2,1)}, bf16[32,48,128]{2,1,0:T(8,128)(2,1)}) custom-call(s32[128]{0:T(128)} %get-tuple-element.61.index_ref, bf16[16,5,8,48,128]{4,3,2,1,0:T(8,128)(2,1)} %bitcast.58), custom_call_target="tpu_custom_call" | custom-call | tf_op jit(solution)/shard_map/along_y/pick_y/pallas_call | solution.py:94
  71.9 3.0 %collective-permute-start = (bf16[32,48,128]{2,1,0:T(8,128)(2,1)}, bf16[32,48,128]{2,1,0:T(8,128)(2,1)S(1)}, u32[]{:S(2)}, u32[]{:S(2)}) collective-permute-start(bf16[32,48,128]{2,1,0:T(8,128)(2,1)} %get-tuple-element.30), channel_id=1, source_target_pairs={{0,192},{64,0},{128,64},{192,128},{1,193},{65,1},{129,65},{193,129... | collective-permute-start | bytes 1179656 | tf_op jit(solution)/shard_map/along_y/ppermute | solution.py:243
  75.6 0.9 collective-permute-start.2
  77.4 3.4 %pick_x.8 = bf16[128,48,128]{2,1,0:T(8,128)(2,1)} custom-call(s32[128]{0:T(128)} %fusion.11.index_ref, bf16[1,1,32,48,128]{4,3,2,1,0:T(8,128)(2,1)} %bitcast.77, bf16[1,1,32,48,128]{4,3,2,1,0:T(8,128)(2,1)} %bitcast.80, bf16[1,1,32,48,128]{4,3,2,1,0:T(8,128)(2,1)} %bitcast.81, bf16[1,1,32,48,128]{4,3,2,1,0:T(8,128)(2,1)} %bitcast.83), custom_call_target="tpu_custom_call" | custom-call | flops 12000000000 | bytes 36000000 | tf_op jit(solution)/shard_map/along_x/pick_x/pallas_call | solution.py:94
  80.9 4.8 %all-to-all-start.2 = ((bf16[128,48,128]{2,1,0:T(8,128)(2,1)}), bf16[128,48,128]{2,1,0:T(8,128)(2,1)S(1)}, u32[]{:S(2)}, u32[]{:S(2)}) async-start(bf16[128,48,128]{2,1,0:T(8,128)(2,1)} %pick_x.8), calls=%async_computation.2 | async-start | bytes 3145728 | tf_op jit(solution)/shard_map/along_x/all_to_all | solution.py:265
  85.7 3.5 %pick_y.9 = (bf16[32,48,128]{2,1,0:T(8,128)(2,1)}, bf16[32,48,128]{2,1,0:T(8,128)(2,1)}, bf16[32,48,128]{2,1,0:T(8,128)(2,1)}, bf16[32,48,128]{2,1,0:T(8,128)(2,1)}) custom-call(s32[128]{0:T(128)} %get-tuple-element.61.index_ref, bf16[16,5,8,48,128]{4,3,2,1,0:T(8,128)(2,1)} %bitcast.59), custom_call_target="tpu_custom_call" | custom-call | tf_op jit(solution)/shard_map/along_y/pick_y/pallas_call | solution.py:94
  89.2 2.4 collective-permute-start.18
  91.6 1.7 collective-permute-start.19
  93.3 3.8 %collective-permute-done.2 = bf16[32,48,128]{2,1,0:T(8,128)(2,1)S(1)} collective-permute-done((bf16[32,48,128]{2,1,0:T(8,128)(2,1)}, bf16[32,48,128]{2,1,0:T(8,128)(2,1)S(1)}, u32[]{:S(2)}, u32[]{:S(2)}) %collective-permute-start.2) | collective-permute-done | bytes 393248 | tf_op jit(solution)/shard_map/along_y/ppermute | solution.py:243
  97.1 0.7 copy-done.19
  97.9 3.4 %pick_x.6 = bf16[128,48,128]{2,1,0:T(8,128)(2,1)} custom-call(s32[128]{0:T(128)} %fusion.11.index_ref, bf16[1,1,32,48,128]{4,3,2,1,0:T(8,128)(2,1)} %bitcast.76, bf16[1,1,32,48,128]{4,3,2,1,0:T(8,128)(2,1)} %bitcast.78, bf16[1,1,32,48,128]{4,3,2,1,0:T(8,128)(2,1)} %bitcast.79, bf16[1,1,32,48,128]{4,3,2,1,0:T(8,128)(2,1)} %bitcast.82), custom_call_target="tpu_custom_call" | custom-call | flops 12000000000 | bytes 36000000 | tf_op jit(solution)/shard_map/along_x/pick_x/pallas_call | solution.py:94
  101.3 3.2 %all-to-all-done.2 = bf16[128,48,128]{2,1,0:T(8,128)(2,1)S(1)} async-done(((bf16[128,48,128]{2,1,0:T(8,128)(2,1)}), bf16[128,48,128]{2,1,0:T(8,128)(2,1)S(1)}, u32[]{:S(2)}, u32[]{:S(2)}) %all-to-all-start.2) | async-done | bytes 1572896 | tf_op jit(solution)/shard_map/along_x/all_to_all | solution.py:265
  104.5 1.2 copy-done.5
  105.7 5.0 %all-to-all-start = ((bf16[128,48,128]{2,1,0:T(8,128)(2,1)}), bf16[128,48,128]{2,1,0:T(8,128)(2,1)S(1)}, u32[]{:S(2)}, u32[]{:S(2)}) async-start(bf16[128,48,128]{2,1,0:T(8,128)(2,1)} %pick_x.6), calls=%async_computation | async-start | bytes 3145728 | tf_op jit(solution)/shard_map/along_x/all_to_all | solution.py:265
  110.7 3.5 %pick_y.10 = (bf16[32,48,128]{2,1,0:T(8,128)(2,1)}, bf16[32,48,128]{2,1,0:T(8,128)(2,1)}, bf16[32,48,128]{2,1,0:T(8,128)(2,1)}, bf16[32,48,128]{2,1,0:T(8,128)(2,1)}) custom-call(s32[128]{0:T(128)} %get-tuple-element.61.index_ref, bf16[16,5,8,48,128]{4,3,2,1,0:T(8,128)(2,1)} %bitcast.60), custom_call_target="tpu_custom_call" | custom-call | tf_op jit(solution)/shard_map/along_y/pick_y/pallas_call | solution.py:94
  114.3 2.4 collective-permute-start.21
  116.6 1.7 collective-permute-start.22
  118.3 3.5 %pick_x.9 = bf16[128,48,128]{2,1,0:T(8,128)(2,1)} custom-call(s32[128]{0:T(128)} %fusion.11.index_ref, bf16[1,1,32,48,128]{4,3,2,1,0:T(8,128)(2,1)} %bitcast.74, bf16[1,1,32,48,128]{4,3,2,1,0:T(8,128)(2,1)} %bitcast.31.refs_1_, bf16[1,1,32,48,128]{4,3,2,1,0:T(8,128)(2,1)} %bitcast.32.refs_2_, bf16[1,1,32,48,128]{4,3,2,1,0:T(8,128)(2,1)} %bitcast.33.refs_3_), custom_call_target="tpu_custom_call" | custom-call | flops 12000000000 | bytes 36000000 | tf_op jit(solution)/shard_map/along_x/pick_x/pallas_call | solution.py:94
  121.8 6.9 %all-to-all-done = bf16[128,48,128]{2,1,0:T(8,128)(2,1)S(1)} async-done(((bf16[128,48,128]{2,1,0:T(8,128)(2,1)}), bf16[128,48,128]{2,1,0:T(8,128)(2,1)S(1)}, u32[]{:S(2)}, u32[]{:S(2)}) %all-to-all-start) | async-done | bytes 1572896 | tf_op jit(solution)/shard_map/along_x/all_to_all | solution.py:265
  128.7 1.2 copy-done.2
  129.9 5.0 %all-to-all-start.3 = ((bf16[128,48,128]{2,1,0:T(8,128)(2,1)}), bf16[128,48,128]{2,1,0:T(8,128)(2,1)S(1)}, u32[]{:S(2)}, u32[]{:S(2)}) async-start(bf16[128,48,128]{2,1,0:T(8,128)(2,1)} %pick_x.9), calls=%async_computation.3 | async-start | bytes 3145728 | tf_op jit(solution)/shard_map/along_x/all_to_all | solution.py:265
  134.9 3.5 %pick_y.11 = (bf16[32,48,128]{2,1,0:T(8,128)(2,1)}, bf16[32,48,128]{2,1,0:T(8,128)(2,1)}, bf16[32,48,128]{2,1,0:T(8,128)(2,1)}, bf16[32,48,128]{2,1,0:T(8,128)(2,1)}) custom-call(s32[128]{0:T(128)} %get-tuple-element.61.index_ref, bf16[16,5,8,48,128]{4,3,2,1,0:T(8,128)(2,1)} %bitcast.61), custom_call_target="tpu_custom_call" | custom-call | tf_op jit(solution)/shard_map/along_y/pick_y/pallas_call | solution.py:94
  138.4 2.4 collective-permute-start.24
  140.8 1.6 collective-permute-start.25
  142.4 3.4 %pick_x.10 = bf16[128,48,128]{2,1,0:T(8,128)(2,1)} custom-call(s32[128]{0:T(128)} %fusion.11.index_ref, bf16[1,1,32,48,128]{4,3,2,1,0:T(8,128)(2,1)} %bitcast.75, bf16[1,1,32,48,128]{4,3,2,1,0:T(8,128)(2,1)} %bitcast.36.refs_1_, bf16[1,1,32,48,128]{4,3,2,1,0:T(8,128)(2,1)} %bitcast.37.refs_2_, bf16[1,1,32,48,128]{4,3,2,1,0:T(8,128)(2,1)} %bitcast.38.refs_3_), custom_call_target="tpu_custom_call" | custom-call | flops 12000000000 | bytes 36000000 | tf_op jit(solution)/shard_map/along_x/pick_x/pallas_call | solution.py:94
  145.8 6.2 %all-to-all-done.3 = bf16[128,48,128]{2,1,0:T(8,128)(2,1)S(1)} async-done(((bf16[128,48,128]{2,1,0:T(8,128)(2,1)}), bf16[128,48,128]{2,1,0:T(8,128)(2,1)S(1)}, u32[]{:S(2)}, u32[]{:S(2)}) %all-to-all-start.3) | async-done | bytes 1572896 | tf_op jit(solution)/shard_map/along_x/all_to_all | solution.py:265
  152.1 5.0 %all-to-all-start.4 = ((bf16[128,48,128]{2,1,0:T(8,128)(2,1)}), bf16[128,48,128]{2,1,0:T(8,128)(2,1)S(1)}, u32[]{:S(2)}, u32[]{:S(2)}) async-start(bf16[128,48,128]{2,1,0:T(8,128)(2,1)} %pick_x.10), calls=%async_computation.4 | async-start | bytes 3145728 | tf_op jit(solution)/shard_map/along_x/all_to_all | solution.py:265
  157.1 3.5 %pick_y.7 = (bf16[32,48,128]{2,1,0:T(8,128)(2,1)}, bf16[32,48,128]{2,1,0:T(8,128)(2,1)}, bf16[32,48,128]{2,1,0:T(8,128)(2,1)}, bf16[32,48,128]{2,1,0:T(8,128)(2,1)}) custom-call(s32[128]{0:T(128)} %get-tuple-element.61.index_ref, bf16[16,5,8,48,128]{4,3,2,1,0:T(8,128)(2,1)} %bitcast.62), custom_call_target="tpu_custom_call" | custom-call | tf_op jit(solution)/shard_map/along_y/pick_y/pallas_call | solution.py:94
  160.6 2.4 collective-permute-start.3
  163.0 1.4 collective-permute-start.4
  164.7 3.4 %pick_x.11 = bf16[128,48,128]{2,1,0:T(8,128)(2,1)} custom-call(s32[128]{0:T(128)} %fusion.11.index_ref, bf16[1,1,32,48,128]{4,3,2,1,0:T(8,128)(2,1)} %bitcast.73, bf16[1,1,32,48,128]{4,3,2,1,0:T(8,128)(2,1)} %bitcast.41.refs_1_, bf16[1,1,32,48,128]{4,3,2,1,0:T(8,128)(2,1)} %bitcast.42.refs_2_, bf16[1,1,32,48,128]{4,3,2,1,0:T(8,128)(2,1)} %bitcast.43.refs_3_), custom_call_target="tpu_custom_call" | custom-call | flops 12000000000 | bytes 36000000 | tf_op jit(solution)/shard_map/along_x/pick_x/pallas_call | solution.py:94
  168.1 5.3 %all-to-all-done.4 = bf16[128,48,128]{2,1,0:T(8,128)(2,1)S(1)} async-done(((bf16[128,48,128]{2,1,0:T(8,128)(2,1)}), bf16[128,48,128]{2,1,0:T(8,128)(2,1)S(1)}, u32[]{:S(2)}, u32[]{:S(2)}) %all-to-all-start.4) | async-done | bytes 1572896 | tf_op jit(solution)/shard_map/along_x/all_to_all | solution.py:265
  173.4 1.2 copy-done.7
  174.6 5.0 %all-to-all-start.5 = ((bf16[128,48,128]{2,1,0:T(8,128)(2,1)}), bf16[128,48,128]{2,1,0:T(8,128)(2,1)S(1)}, u32[]{:S(2)}, u32[]{:S(2)}) async-start(bf16[128,48,128]{2,1,0:T(8,128)(2,1)} %pick_x.11), calls=%async_computation.5 | async-start | bytes 3145728 | tf_op jit(solution)/shard_map/along_x/all_to_all | solution.py:265
  179.6 0.8 dynamic_slice.24
  180.4 3.5 %pick_x.7 = bf16[128,48,128]{2,1,0:T(8,128)(2,1)} custom-call(s32[128]{0:T(128)} %fusion.11.index_ref, bf16[1,1,32,48,128]{4,3,2,1,0:T(8,128)(2,1)} %bitcast.72, bf16[1,1,32,48,128]{4,3,2,1,0:T(8,128)(2,1)} %bitcast.13.refs_1_, bf16[1,1,32,48,128]{4,3,2,1,0:T(8,128)(2,1)} %bitcast.14.refs_2_, bf16[1,1,32,48,128]{4,3,2,1,0:T(8,128)(2,1)} %bitcast.15.refs_3_), custom_call_target="tpu_custom_call" | custom-call | flops 12000000000 | bytes 36000000 | tf_op jit(solution)/shard_map/along_x/pick_x/pallas_call | solution.py:94
  183.9 11.3 %all-to-all-done.5 = bf16[128,48,128]{2,1,0:T(8,128)(2,1)S(1)} async-done(((bf16[128,48,128]{2,1,0:T(8,128)(2,1)}), bf16[128,48,128]{2,1,0:T(8,128)(2,1)S(1)}, u32[]{:S(2)}, u32[]{:S(2)}) %all-to-all-start.5) | async-done | bytes 1572896 | tf_op jit(solution)/shard_map/along_x/all_to_all | solution.py:265
  195.2 1.1 copy-done.8
  196.3 5.0 %all-to-all-start.1 = ((bf16[128,48,128]{2,1,0:T(8,128)(2,1)}), bf16[128,48,128]{2,1,0:T(8,128)(2,1)S(1)}, u32[]{:S(2)}, u32[]{:S(2)}) async-start(bf16[128,48,128]{2,1,0:T(8,128)(2,1)} %pick_x.7), calls=%async_computation.1 | async-start | bytes 3145728 | tf_op jit(solution)/shard_map/along_x/all_to_all | solution.py:265
  202.0 14.3 %couple.2.rest_2_ = f32[8,384,384]{2,1,0:T(8,128)} custom-call(s32[32]{0:T(128)} %and_select_fusion.4.target, f32[32]{0:T(128)} %fock.3, bf16[32,384,384]{2,1,0:T(8,128)(2,1)} %s_ref.3, bf16[4,32,48,128]{3,2,1,0:T(8,128)(2,1)} %bitcast.65, bf16[4,32,48,128]{3,2,1,0:T(8,128)(2,1)} %bitcast.66, bf16[4,32,48,128]{3,2,1,0:T(8,128)(2,1)} %bitcast.67, ...), custom_call_target="tpu_custom_call" | custom-call | flops 9663676416 | bytes 14155776 | tf_op jit(solution)/shard_map/couple/couple/pallas_call | solution.py:276
  216.3 1.2 copy-done.3
  217.5 13.8 %couple.3 = bf16[4,8,96,384]{3,2,1,0:T(8,128)(2,1)} custom-call(s32[32]{0:T(128)} %and_select_fusion.4.target, f32[32]{0:T(128)} %fock.3, bf16[32,384,384]{2,1,0:T(8,128)(2,1)} %s_ref.3, bf16[4,32,48,128]{3,2,1,0:T(8,128)(2,1)} %bitcast.63, bf16[4,32,48,128]{3,2,1,0:T(8,128)(2,1)} %bitcast.64, f32[8,384,384]{2,1,0:T(8,128)} %couple.2.rest_2_), custom_call_target="tpu_custom_call" | custom-call | flops 4831838208 | bytes 14155776 | tf_op jit(solution)/shard_map/couple/couple/pallas_call | solution.py:276
  231.3 4.9 %all-to-all-start.6 = ((bf16[4,8,96,384]{3,2,1,0:T(8,128)(2,1)}), bf16[4,8,96,384]{3,2,1,0:T(8,128)(2,1)S(1)}, u32[]{:S(2)}, u32[]{:S(2)}) async-start(bf16[4,8,96,384]{3,2,1,0:T(8,128)(2,1)} %couple.3), calls=%async_computation.6 | async-start | bytes 4718592 | tf_op jit(solution)/shard_map/sum_x/all_to_all | solution.py:278
  236.3 22.1 %all-to-all-done.6 = bf16[4,8,96,384]{3,2,1,0:T(8,128)(2,1)S(1)} async-done(((bf16[4,8,96,384]{3,2,1,0:T(8,128)(2,1)}), bf16[4,8,96,384]{3,2,1,0:T(8,128)(2,1)S(1)}, u32[]{:S(2)}, u32[]{:S(2)}) %all-to-all-start.6) | async-done | bytes 2359328 | tf_op jit(solution)/shard_map/sum_x/all_to_all | solution.py:278
  259.5 1.9 convert_subtract_fusion
  (103 shorter events, 7.4 us)
Async XLA Ops:
  7.2 8.2 %copy-start = (s32[8192]{0:T(1024)S(1)}, s32[8192]{0:T(1024)}, u32[]{:S(2)}) copy-start(s32[8192]{0:T(1024)} %param.15) | copy-start | bytes 98308
  7.2 61.2 %all-gather.3.cloned.1.call-start = ((), (), s32[]{:S(2)}) async-start(), calls=%async_computation.7 | async-start | bytes 8355840 | tf_op jit(solution)/shard_map/along_z/all_gather | solution.py:255
  9.3 9.1 %collective-permute-start.6 = (bf16[1,8,48,128]{3,2,1,0:T(8,128)(2,1)}, bf16[1,8,48,128]{3,2,1,0:T(8,128)(2,1)S(1)}, u32[]{:S(2)}, u32[]{:S(2)}) collective-permute-start(bf16[1,8,48,128]{3,2,1,0:T(8,128)(2,1)} %get-tuple-element.37), channel_id=1, source_target_pairs={{0,8},{8,16},{16,24},{24,32},{32,40},{40,48},{48,56},{56,0},{1,9},... | collective-permute-start | bytes 294920 | tf_op jit(solution)/shard_map/along_z/ppermute | solution.py:33
  11.3 7.2 %collective-permute-start.7 = (bf16[1,8,48,128]{3,2,1,0:T(8,128)(2,1)}, bf16[1,8,48,128]{3,2,1,0:T(8,128)(2,1)S(1)}, u32[]{:S(2)}, u32[]{:S(2)}) collective-permute-start(bf16[1,8,48,128]{3,2,1,0:T(8,128)(2,1)} %get-tuple-element.37), channel_id=1, source_target_pairs={{0,56},{8,0},{16,8},{24,16},{32,24},{40,32},{48,40},{56,48},{1,57}... | collective-permute-start | bytes 294920 | tf_op jit(solution)/shard_map/along_z/ppermute | solution.py:34
  18.4 5.9 %collective-permute-start.8 = (bf16[1,8,48,128]{3,2,1,0:T(8,128)(2,1)S(1)}, bf16[1,8,48,128]{3,2,1,0:T(8,128)(2,1)S(1)}, u32[]{:S(2)}, u32[]{:S(2)}) collective-permute-start(bf16[1,8,48,128]{3,2,1,0:T(8,128)(2,1)S(1)} %collective-permute-done.6), channel_id=1, source_target_pairs={{0,8},{8,16},{16,24},{24,32},{32,40},{40,48},{48,56},{56,0},{1,9},... | collective-permute-start | bytes 294920 | tf_op jit(solution)/shard_map/along_z/ppermute | solution.py:33
  18.5 5.8 %collective-permute-start.9 = (bf16[1,8,48,128]{3,2,1,0:T(8,128)(2,1)S(1)}, bf16[1,8,48,128]{3,2,1,0:T(8,128)(2,1)S(1)}, u32[]{:S(2)}, u32[]{:S(2)}) collective-permute-start(bf16[1,8,48,128]{3,2,1,0:T(8,128)(2,1)S(1)} %collective-permute-done.7), channel_id=1, source_target_pairs={{0,56},{8,0},{16,8},{24,16},{32,24},{40,32},{48,40},{56,48},{1,57}... | collective-permute-start | bytes 294920 | tf_op jit(solution)/shard_map/along_z/ppermute | solution.py:34
  24.3 11.2 %collective-permute-start.10 = (bf16[1,8,48,128]{3,2,1,0:T(8,128)(2,1)S(1)}, bf16[1,8,48,128]{3,2,1,0:T(8,128)(2,1)S(1)}, u32[]{:S(2)}, u32[]{:S(2)}) collective-permute-start(bf16[1,8,48,128]{3,2,1,0:T(8,128)(2,1)S(1)} %collective-permute-done.8), channel_id=1, source_target_pairs={{0,8},{8,16},{16,24},{24,32},{32,40},{40,48},{48,56},{56,0},{1,9},... | collective-permute-start | bytes 294920 | tf_op jit(solution)/shard_map/along_z/ppermute | solution.py:33
  24.3 7.5 %collective-permute-start.11 = (bf16[1,8,48,128]{3,2,1,0:T(8,128)(2,1)S(1)}, bf16[1,8,48,128]{3,2,1,0:T(8,128)(2,1)S(1)}, u32[]{:S(2)}, u32[]{:S(2)}) collective-permute-start(bf16[1,8,48,128]{3,2,1,0:T(8,128)(2,1)S(1)} %collective-permute-done.9), channel_id=1, source_target_pairs={{0,56},{8,0},{16,8},{24,16},{32,24},{40,32},{48,40},{56,48},{1,57}... | collective-permute-start | bytes 294920 | tf_op jit(solution)/shard_map/along_z/ppermute | solution.py:34
  31.8 6.3 %collective-permute-start.13 = (bf16[1,4,48,128]{3,2,1,0:T(8,128)(2,1)S(1)}, bf16[1,4,48,128]{3,2,1,0:T(8,128)(2,1)S(1)}, u32[]{:S(2)}, u32[]{:S(2)}) collective-permute-start(bf16[1,4,48,128]{3,2,1,0:T(8,128)(2,1)S(1)} %slice.9), channel_id=1, source_target_pairs={{0,56},{8,0},{16,8},{24,16},{32,24},{40,32},{48,40},{56,48},{1,57}... | collective-permute-start | bytes 147464 | tf_op jit(solution)/shard_map/along_z/ppermute | solution.py:38
  35.5 6.4 %collective-permute-start.12 = (bf16[1,4,48,128]{3,2,1,0:T(8,128)(2,1)S(1)}, bf16[1,4,48,128]{3,2,1,0:T(8,128)(2,1)S(1)}, u32[]{:S(2)}, u32[]{:S(2)}) collective-permute-start(bf16[1,4,48,128]{3,2,1,0:T(8,128)(2,1)S(1)} %slice.8), channel_id=1, source_target_pairs={{0,8},{8,16},{16,24},{24,32},{32,40},{40,48},{48,56},{56,0},{1,9},... | collective-permute-start | bytes 147464 | tf_op jit(solution)/shard_map/along_z/ppermute | solution.py:37
  41.9 2.4 copy-start.9
  42.0 2.4 collective-permute-start.14
  44.3 0.9 copy-start.10
  48.8 26.7 %collective-permute-start.15 = (bf16[32,48,128]{2,1,0:T(8,128)(2,1)}, bf16[32,48,128]{2,1,0:T(8,128)(2,1)S(1)}, u32[]{:S(2)}, u32[]{:S(2)}) collective-permute-start(bf16[32,48,128]{2,1,0:T(8,128)(2,1)} %get-tuple-element.39), channel_id=1, source_target_pairs={{0,192},{64,0},{128,64},{192,128},{1,193},{65,1},{129,65},{193,129... | collective-permute-start | bytes 1179656 | tf_op jit(solution)/shard_map/along_y/ppermute | solution.py:243
  52.1 24.4 %collective-permute-start.16 = (bf16[32,48,128]{2,1,0:T(8,128)(2,1)}, bf16[32,48,128]{2,1,0:T(8,128)(2,1)S(1)}, u32[]{:S(2)}, u32[]{:S(2)}) collective-permute-start(bf16[32,48,128]{2,1,0:T(8,128)(2,1)} %get-tuple-element.40), channel_id=1, source_target_pairs={{0,128},{64,192},{128,0},{192,64},{1,129},{65,193},{129,1},{193,65... | collective-permute-start | bytes 1179656 | tf_op jit(solution)/shard_map/along_y/ppermute | solution.py:243
  52.6 23.9 %collective-permute-start.17 = (bf16[32,48,128]{2,1,0:T(8,128)(2,1)}, bf16[32,48,128]{2,1,0:T(8,128)(2,1)S(1)}, u32[]{:S(2)}, u32[]{:S(2)}) collective-permute-start(bf16[32,48,128]{2,1,0:T(8,128)(2,1)} %get-tuple-element.41), channel_id=1, source_target_pairs={{0,64},{64,128},{128,192},{192,0},{1,65},{65,129},{129,193},{193,1... | collective-permute-start | bytes 1179656 | tf_op jit(solution)/shard_map/along_y/ppermute | solution.py:243
  71.9 21.3 %collective-permute-start = (bf16[32,48,128]{2,1,0:T(8,128)(2,1)}, bf16[32,48,128]{2,1,0:T(8,128)(2,1)S(1)}, u32[]{:S(2)}, u32[]{:S(2)}) collective-permute-start(bf16[32,48,128]{2,1,0:T(8,128)(2,1)} %get-tuple-element.30), channel_id=1, source_target_pairs={{0,192},{64,0},{128,64},{192,128},{1,193},{65,1},{129,65},{193,129... | collective-permute-start | bytes 1179656 | tf_op jit(solution)/shard_map/along_y/ppermute | solution.py:243
  74.9 18.4 %collective-permute-start.1 = (bf16[32,48,128]{2,1,0:T(8,128)(2,1)}, bf16[32,48,128]{2,1,0:T(8,128)(2,1)S(1)}, u32[]{:S(2)}, u32[]{:S(2)}) collective-permute-start(bf16[32,48,128]{2,1,0:T(8,128)(2,1)} %get-tuple-element.31), channel_id=1, source_target_pairs={{0,128},{64,192},{128,0},{192,64},{1,129},{65,193},{129,1},{193,65... | collective-permute-start | bytes 1179656 | tf_op jit(solution)/shard_map/along_y/ppermute | solution.py:243
  75.6 0.9 copy-start.17
  75.6 21.5 %collective-permute-start.2 = (bf16[32,48,128]{2,1,0:T(8,128)(2,1)}, bf16[32,48,128]{2,1,0:T(8,128)(2,1)S(1)}, u32[]{:S(2)}, u32[]{:S(2)}) collective-permute-start(bf16[32,48,128]{2,1,0:T(8,128)(2,1)} %get-tuple-element.32), channel_id=1, source_target_pairs={{0,64},{64,128},{128,192},{192,0},{1,65},{65,129},{129,193},{193,1... | collective-permute-start | bytes 1179656 | tf_op jit(solution)/shard_map/along_y/ppermute | solution.py:243
  76.5 0.8 copy-start.18
  76.5 0.9 copy-start.20
  80.9 23.7 %all-to-all-start.2 = ((bf16[128,48,128]{2,1,0:T(8,128)(2,1)}), bf16[128,48,128]{2,1,0:T(8,128)(2,1)S(1)}, u32[]{:S(2)}, u32[]{:S(2)}) async-start(bf16[128,48,128]{2,1,0:T(8,128)(2,1)} %pick_x.8), calls=%async_computation.2 | async-start | bytes 3145728 | tf_op jit(solution)/shard_map/along_x/all_to_all | solution.py:265
  89.2 29.1 %collective-permute-start.18 = (bf16[32,48,128]{2,1,0:T(8,128)(2,1)}, bf16[32,48,128]{2,1,0:T(8,128)(2,1)}, u32[]{:S(2)}, u32[]{:S(2)}) collective-permute-start(bf16[32,48,128]{2,1,0:T(8,128)(2,1)} %get-tuple-element.43), channel_id=1, source_target_pairs={{0,192},{64,0},{128,64},{192,128},{1,193},{65,1},{129,65},{193,129... | collective-permute-start | bytes 1179656 | tf_op jit(solution)/shard_map/along_y/ppermute | solution.py:243
  91.6 26.7 %collective-permute-start.19 = (bf16[32,48,128]{2,1,0:T(8,128)(2,1)}, bf16[32,48,128]{2,1,0:T(8,128)(2,1)}, u32[]{:S(2)}, u32[]{:S(2)}) collective-permute-start(bf16[32,48,128]{2,1,0:T(8,128)(2,1)} %get-tuple-element.44), channel_id=1, source_target_pairs={{0,128},{64,192},{128,0},{192,64},{1,129},{65,193},{129,1},{193,65... | collective-permute-start | bytes 1179656 | tf_op jit(solution)/shard_map/along_y/ppermute | solution.py:243
  93.3 3.9 %copy-start.15 = (bf16[32,48,128]{2,1,0:T(8,128)(2,1)}, bf16[32,48,128]{2,1,0:T(8,128)(2,1)S(1)}, u32[]{:S(2)}) copy-start(bf16[32,48,128]{2,1,0:T(8,128)(2,1)S(1)} %collective-permute-done) | copy-start | bytes 1179652
  93.3 25.1 %collective-permute-start.20 = (bf16[32,48,128]{2,1,0:T(8,128)(2,1)}, bf16[32,48,128]{2,1,0:T(8,128)(2,1)}, u32[]{:S(2)}, u32[]{:S(2)}) collective-permute-start(bf16[32,48,128]{2,1,0:T(8,128)(2,1)} %get-tuple-element.45), channel_id=1, source_target_pairs={{0,64},{64,128},{128,192},{192,0},{1,65},{65,129},{129,193},{193,1... | collective-permute-start | bytes 1179656 | tf_op jit(solution)/shard_map/along_y/ppermute | solution.py:243
  93.3 3.8 %copy-start.16 = (bf16[32,48,128]{2,1,0:T(8,128)(2,1)}, bf16[32,48,128]{2,1,0:T(8,128)(2,1)S(1)}, u32[]{:S(2)}) copy-start(bf16[32,48,128]{2,1,0:T(8,128)(2,1)S(1)} %collective-permute-done.1) | copy-start | bytes 1179652
  97.1 0.7 copy-start.19
  104.5 1.2 copy-start.5
  105.7 23.0 %all-to-all-start = ((bf16[128,48,128]{2,1,0:T(8,128)(2,1)}), bf16[128,48,128]{2,1,0:T(8,128)(2,1)S(1)}, u32[]{:S(2)}, u32[]{:S(2)}) async-start(bf16[128,48,128]{2,1,0:T(8,128)(2,1)} %pick_x.6), calls=%async_computation | async-start | bytes 3145728 | tf_op jit(solution)/shard_map/along_x/all_to_all | solution.py:265
  114.3 28.1 %collective-permute-start.21 = (bf16[32,48,128]{2,1,0:T(8,128)(2,1)}, bf16[32,48,128]{2,1,0:T(8,128)(2,1)}, u32[]{:S(2)}, u32[]{:S(2)}) collective-permute-start(bf16[32,48,128]{2,1,0:T(8,128)(2,1)} %get-tuple-element.47), channel_id=1, source_target_pairs={{0,192},{64,0},{128,64},{192,128},{1,193},{65,1},{129,65},{193,129... | collective-permute-start | bytes 1179656 | tf_op jit(solution)/shard_map/along_y/ppermute | solution.py:243
  116.6 25.8 %collective-permute-start.22 = (bf16[32,48,128]{2,1,0:T(8,128)(2,1)}, bf16[32,48,128]{2,1,0:T(8,128)(2,1)}, u32[]{:S(2)}, u32[]{:S(2)}) collective-permute-start(bf16[32,48,128]{2,1,0:T(8,128)(2,1)} %get-tuple-element.48), channel_id=1, source_target_pairs={{0,128},{64,192},{128,0},{192,64},{1,129},{65,193},{129,1},{193,65... | collective-permute-start | bytes 1179656 | tf_op jit(solution)/shard_map/along_y/ppermute | solution.py:243
  118.3 24.1 %collective-permute-start.23 = (bf16[32,48,128]{2,1,0:T(8,128)(2,1)}, bf16[32,48,128]{2,1,0:T(8,128)(2,1)}, u32[]{:S(2)}, u32[]{:S(2)}) collective-permute-start(bf16[32,48,128]{2,1,0:T(8,128)(2,1)} %get-tuple-element.49), channel_id=1, source_target_pairs={{0,64},{64,128},{128,192},{192,0},{1,65},{65,129},{129,193},{193,1... | collective-permute-start | bytes 1179656 | tf_op jit(solution)/shard_map/along_y/ppermute | solution.py:243
  128.7 1.2 copy-start.2
  129.9 22.2 %all-to-all-start.3 = ((bf16[128,48,128]{2,1,0:T(8,128)(2,1)}), bf16[128,48,128]{2,1,0:T(8,128)(2,1)S(1)}, u32[]{:S(2)}, u32[]{:S(2)}) async-start(bf16[128,48,128]{2,1,0:T(8,128)(2,1)} %pick_x.9), calls=%async_computation.3 | async-start | bytes 3145728 | tf_op jit(solution)/shard_map/along_x/all_to_all | solution.py:265
  138.4 25.9 %collective-permute-start.24 = (bf16[32,48,128]{2,1,0:T(8,128)(2,1)}, bf16[32,48,128]{2,1,0:T(8,128)(2,1)}, u32[]{:S(2)}, u32[]{:S(2)}) collective-permute-start(bf16[32,48,128]{2,1,0:T(8,128)(2,1)} %get-tuple-element.51), channel_id=1, source_target_pairs={{0,192},{64,0},{128,64},{192,128},{1,193},{65,1},{129,65},{193,129... | collective-permute-start | bytes 1179656 | tf_op jit(solution)/shard_map/along_y/ppermute | solution.py:243
  140.8 23.9 %collective-permute-start.25 = (bf16[32,48,128]{2,1,0:T(8,128)(2,1)}, bf16[32,48,128]{2,1,0:T(8,128)(2,1)}, u32[]{:S(2)}, u32[]{:S(2)}) collective-permute-start(bf16[32,48,128]{2,1,0:T(8,128)(2,1)} %get-tuple-element.52), channel_id=1, source_target_pairs={{0,128},{64,192},{128,0},{192,64},{1,129},{65,193},{129,1},{193,65... | collective-permute-start | bytes 1179656 | tf_op jit(solution)/shard_map/along_y/ppermute | solution.py:243
  142.3 22.4 %collective-permute-start.26 = (bf16[32,48,128]{2,1,0:T(8,128)(2,1)}, bf16[32,48,128]{2,1,0:T(8,128)(2,1)}, u32[]{:S(2)}, u32[]{:S(2)}) collective-permute-start(bf16[32,48,128]{2,1,0:T(8,128)(2,1)} %get-tuple-element.53), channel_id=1, source_target_pairs={{0,64},{64,128},{128,192},{192,0},{1,65},{65,129},{129,193},{193,1... | collective-permute-start | bytes 1179656 | tf_op jit(solution)/shard_map/along_y/ppermute | solution.py:243
  152.1 8.5 %copy-start.6 = (bf16[128,48,128]{2,1,0:T(8,128)(2,1)}, bf16[128,48,128]{2,1,0:T(8,128)(2,1)S(1)}, u32[]{:S(2)}) copy-start(bf16[128,48,128]{2,1,0:T(8,128)(2,1)S(1)} %all-to-all-done.3) | copy-start | bytes 4718596
  152.1 21.4 %all-to-all-start.4 = ((bf16[128,48,128]{2,1,0:T(8,128)(2,1)}), bf16[128,48,128]{2,1,0:T(8,128)(2,1)S(1)}, u32[]{:S(2)}, u32[]{:S(2)}) async-start(bf16[128,48,128]{2,1,0:T(8,128)(2,1)} %pick_x.10), calls=%async_computation.4 | async-start | bytes 3145728 | tf_op jit(solution)/shard_map/along_x/all_to_all | solution.py:265
  160.6 19.7 %collective-permute-start.3 = (bf16[32,48,128]{2,1,0:T(8,128)(2,1)}, bf16[32,48,128]{2,1,0:T(8,128)(2,1)}, u32[]{:S(2)}, u32[]{:S(2)}) collective-permute-start(bf16[32,48,128]{2,1,0:T(8,128)(2,1)} %get-tuple-element.34), channel_id=1, source_target_pairs={{0,192},{64,0},{128,64},{192,128},{1,193},{65,1},{129,65},{193,129... | collective-permute-start | bytes 1179656 | tf_op jit(solution)/shard_map/along_y/ppermute | solution.py:243
  163.0 17.4 %collective-permute-start.4 = (bf16[32,48,128]{2,1,0:T(8,128)(2,1)}, bf16[32,48,128]{2,1,0:T(8,128)(2,1)}, u32[]{:S(2)}, u32[]{:S(2)}) collective-permute-start(bf16[32,48,128]{2,1,0:T(8,128)(2,1)} %get-tuple-element.35), channel_id=1, source_target_pairs={{0,128},{64,192},{128,0},{192,64},{1,129},{65,193},{129,1},{193,65... | collective-permute-start | bytes 1179656 | tf_op jit(solution)/shard_map/along_y/ppermute | solution.py:243
  164.3 16.0 %collective-permute-start.5 = (bf16[32,48,128]{2,1,0:T(8,128)(2,1)}, bf16[32,48,128]{2,1,0:T(8,128)(2,1)}, u32[]{:S(2)}, u32[]{:S(2)}) collective-permute-start(bf16[32,48,128]{2,1,0:T(8,128)(2,1)} %get-tuple-element.36), channel_id=1, source_target_pairs={{0,64},{64,128},{128,192},{192,0},{1,65},{65,129},{129,193},{193,1... | collective-permute-start | bytes 1179656 | tf_op jit(solution)/shard_map/along_y/ppermute | solution.py:243
  173.4 1.2 copy-start.7
  174.6 20.6 %all-to-all-start.5 = ((bf16[128,48,128]{2,1,0:T(8,128)(2,1)}), bf16[128,48,128]{2,1,0:T(8,128)(2,1)S(1)}, u32[]{:S(2)}, u32[]{:S(2)}) async-start(bf16[128,48,128]{2,1,0:T(8,128)(2,1)} %pick_x.11), calls=%async_computation.5 | async-start | bytes 3145728 | tf_op jit(solution)/shard_map/along_x/all_to_all | solution.py:265
  183.8 17.5 %copy-start.13 = (s32[512]{0:T(512)S(1)}, s32[512]{0:T(512)}, u32[]{:S(2)}) copy-start(s32[512]{0:T(512)} %param.14) | copy-start | bytes 6148
  195.2 1.2 copy-start.8
  196.3 20.0 %all-to-all-start.1 = ((bf16[128,48,128]{2,1,0:T(8,128)(2,1)}), bf16[128,48,128]{2,1,0:T(8,128)(2,1)S(1)}, u32[]{:S(2)}, u32[]{:S(2)}) async-start(bf16[128,48,128]{2,1,0:T(8,128)(2,1)} %pick_x.7), calls=%async_computation.1 | async-start | bytes 3145728 | tf_op jit(solution)/shard_map/along_x/all_to_all | solution.py:265
  216.3 1.2 copy-start.3
  231.3 4.9 %copy-start.12 = (f32[8,384]{1,0:T(8,128)S(1)}, f32[8,384]{1,0:T(8,128)}, u32[]{:S(2)}) copy-start(f32[8,384]{1,0:T(8,128)} %param.12) | copy-start | bytes 36868
  231.3 27.1 %all-to-all-start.6 = ((bf16[4,8,96,384]{3,2,1,0:T(8,128)(2,1)}), bf16[4,8,96,384]{3,2,1,0:T(8,128)(2,1)S(1)}, u32[]{:S(2)}, u32[]{:S(2)}) async-start(bf16[4,8,96,384]{3,2,1,0:T(8,128)(2,1)} %couple.3), calls=%async_computation.6 | async-start | bytes 4718592 | tf_op jit(solution)/shard_map/sum_x/all_to_all | solution.py:278
  236.3 22.5 %copy-start.4 = (bf16[8,96,384]{2,1,0:T(8,128)(2,1)S(1)}, bf16[8,96,384]{2,1,0:T(8,128)(2,1)}, u32[]{:S(2)}) copy-start(bf16[8,96,384]{2,1,0:T(8,128)(2,1)} %in_ref.1) | copy-start | bytes 1769476
  236.3 22.5 %copy-start.14 = (f32[8]{0:T(128)S(1)}, f32[8]{0:T(128)}, u32[]{:S(2)}) copy-start(f32[8]{0:T(128)} %param.13) | copy-start | bytes 100
  258.4 1.1 copy-start.11
  258.4 3.0 %copy-start.1 = (s32[8192]{0:T(1024)S(1)}, s32[8192]{0:T(1024)}, u32[]{:S(2)}) copy-start(s32[8192]{0:T(1024)} %param.15) | copy-start | bytes 98308
Sparse Core Ops, SparseCore 0:
  9.8 58.4 all-gather.2

commit v2 on v1

--- a/solution.py
+++ b/solution.py
@@ -12,7 +12,7 @@
     ("gather", ((0, 1), (1, 0), (1, 1), (2, 0), (2, 1))),
 )
 STAGES = ((0, 1), (2,))
-UNROLL = 4
+UNROLL = 8
 RING_PLACE = (0, 2, 4, 6, 7, 5, 3, 1)
 STAGE_FLOPS = 12_000_000_000
 STAGE_BYTES = 36_000_000
@@ -40,23 +40,19 @@
     return jnp.stack(parts)
 
 
-def split(amplitude, piece):
+def split(amplitude, piece, members):
     pairs, _, _ = amplitude.shape
 
-    def kernel(in_ref, *out_refs):
-        for out_ref, (_, members) in zip(out_refs, GROUPS):
-            for n, (j, r) in enumerate(members):
-                rows = slice(r * piece, (r + 1) * piece)
-                lanes = slice(j * COLUMNS, (j + 1) * COLUMNS)
-                for p in range(pairs):
-                    out_ref[n, p] = in_ref[p, rows, lanes]
+    def kernel(in_ref, out_ref):
+        for n, (j, r) in enumerate(members):
+            rows = slice(r * piece, (r + 1) * piece)
+            lanes = slice(j * COLUMNS, (j + 1) * COLUMNS)
+            for p in range(pairs):
+                out_ref[n, p] = in_ref[p, rows, lanes]
 
     return pl.pallas_call(
         kernel,
-        out_shape=[
-            jax.ShapeDtypeStruct((len(members), pairs, piece, COLUMNS), amplitude.dtype)
-            for _, members in GROUPS
-        ],
+        out_shape=jax.ShapeDtypeStruct((len(members), pairs, piece, COLUMNS), amplitude.dtype),
         name="split",
     )(amplitude)
 
@@ -100,7 +96,7 @@
             pltpu.VMEM((sum(sizes), piece, lanes), arrays[0].dtype),
             pltpu.SemaphoreType.DMA((sum(array.shape[0] for array in arrays),)),
         ],
-        compiler_params=pltpu.CompilerParams(vmem_limit_bytes=60 * 1024 * 1024),
+        compiler_params=pltpu.CompilerParams(vmem_limit_bytes=52 * 1024 * 1024),
         cost_estimate=cost,
         name=name,
     )(index, *arrays)
@@ -120,14 +116,15 @@
         out_ref = rest.pop(0)
         acc = rest.pop(0) if final else out_ref
         step = pl.program_id(0)
+        fill = None if first else pltpu.make_async_copy(base_ref, acc, rest.pop(0))
 
         @pl.when(step == 0)
         def _():
-            for p in range(pairs):
-                if first:
+            if first:
+                for p in range(pairs):
                     acc[p] = jnp.zeros((width, width), jnp.float32)
-                else:
-                    acc[p] = base_ref[p]
+            else:
+                fill.start()
 
         lefts = []
         for g in range(UNROLL):
@@ -138,6 +135,12 @@
             amp = strips[0] if len(strips) == 1 else jnp.concatenate(strips, axis=1)
             left = jnp.dot(s_ref[g], amp, preferred_element_type=jnp.float32)
             lefts.append(left.astype(jnp.bfloat16))
+        if not first:
+
+            @pl.when(step == 0)
+            def _():
+                fill.wait()
+
         for g in range(UNROLL):
             part = lax.dot_general(
                 lefts[g],
@@ -159,12 +162,14 @@
     in_specs = [pl.BlockSpec((UNROLL, width, width), lambda i, *_: (i, 0, 0))]
     in_specs += [pl.BlockSpec((quarters, UNROLL, piece, COLUMNS), lambda i, *_: (0, i, 0, 0))] * blocks
     if not first:
-        in_specs.append(whole)
+        in_specs.append(pl.BlockSpec(memory_space=pl.ANY))
     scratch = []
     if final:
         out_shape = jax.ShapeDtypeStruct((quarters, pairs, rows, width), jnp.bfloat16)
         out_specs = pl.BlockSpec((quarters, pairs, rows, width), lambda i, *_: (0, 0, 0, 0))
         scratch.append(pltpu.VMEM((pairs, width, width), jnp.float32))
+        if not first:
+            scratch.append(pltpu.SemaphoreType.DMA)
     else:
         out_shape = jax.ShapeDtypeStruct((pairs, width, width), jnp.float32)
         out_specs = whole
@@ -178,7 +183,7 @@
             scratch_shapes=scratch,
         ),
         out_shape=out_shape,
-        compiler_params=pltpu.CompilerParams(vmem_limit_bytes=60 * 1024 * 1024),
+        compiler_params=pltpu.CompilerParams(vmem_limit_bytes=52 * 1024 * 1024),
         cost_estimate=pl.CostEstimate(
             flops=8 * count * width * width * columns,
             bytes_accessed=count * width * width * 3,
@@ -244,8 +249,8 @@
 
     stage_cost = pl.CostEstimate(flops=STAGE_FLOPS, bytes_accessed=STAGE_BYTES, transcendentals=0)
     landed = {}
-    blocks = split(amplitude, piece)
-    for (kind, members), block in zip(GROUPS, blocks):
+    for kind, members in GROUPS:
+        block = split(amplitude, piece, members)
         with jax.named_scope("along_z"):
             if kind == "ring":
                 own = ring_gather(block)

time: 270 us -> 263 us (0.974)
  local copies, waits for them, and re-layouts: 11.7 us -> 5.7 us
  Pallas kernels: 72 us -> 67.6 us
  waiting for transfers between devices: 86.9 us -> 90.5 us
  starting transfers between devices: 76.7 us -> 79.7 us
  other arithmetic: 6.55 us -> 3.59 us
    unnamed x49 -> x37, local copies, waits for them, and re-layouts: 10.1 us -> 4.15 us
    pallas_call x2, Pallas kernels: 28.1 us -> 24.6 us  [per_device(): total = couple(*args)]
    all_to_all x6, starting transfers between devices: 29.8 us -> 32.9 us  [per_device(): arrived = lax.all_to_all(leaving, 'dom', 0, 0, tiled=True)]
  transfers between devices with their start and end apart: 35 -> 35, of which waited for: 13 -> 17; matrix products, arithmetic and copies ran while one was open for 3% -> 1% of each run, Pallas kernels for 21% -> 20%
where the time goes in v2:
time: 263 us; the launch traced here: 261 us
  waiting for transfers between devices  90.5 us (34%)
  starting transfers between devices  79.7 us (30%)
  Pallas kernels  67.6 us (26%)
  between operations  14.4 us (5%)
  local copies, waits for them, and re-layouts  5.7 us (2%)
  other arithmetic  3.59 us (1%)
    pallas_call x12, Pallas kernels, pick(): pl.pallas_call(kernel, in_specs=[pl.BlockSpec(memory_space=pltpu.SMEM)] +...  39.3 us
    all_to_all x6, waiting for transfers between devices, per_device(): arrived = lax.all_to_all(leaving, 'dom', 0, 0, tiled=True)  33.6 us
    all_to_all x6, starting transfers between devices, per_device(): arrived = lax.all_to_all(leaving, 'dom', 0, 0, tiled=True)  32.9 us
    ppermute x18, starting transfers between devices, shift(): return lax.ppermute(array, 'y', [(i, (i + step) % ny) for i in range(ny)])  25 us
    pallas_call x2, Pallas kernels, per_device(): total = couple(*args)  24.6 us
    all_to_all x1, waiting for transfers between devices, per_device(): shares = lax.all_to_all(total, 'dom', 0, 0, tiled=True)  21.3 us
    all_gather x1, waiting for transfers between devices, per_device(): around, index = ([lax.all_gather(block, ('z', 'core'), axis=0)], all_index)  12.2 us
    ppermute x3, starting transfers between devices, ring_gather(): below = lax.ppermute(below, 'z', down)  10.9 us
  transfers between devices with their start and end apart: 35, of which 17 were waited for; matrix products, arithmetic and copies ran while one was open for 1% of the time, Pallas kernels for 20%

profile of v2, /device:TPU:2, one launch (start us, length us, event | category | flops | bytes accessed | tf_op | source)
XLA Modules:
  0.0 261.5 jit_solution(11292815896601778452)
XLA Ops:
  7.2 2.0 split.2
  9.2 1.7 split.3
  11.0 1.9 collective-permute-start.6
  12.9 3.9 %collective-permute-start.7 = (bf16[1,8,48,128]{3,2,1,0:T(8,128)(2,1)}, bf16[1,8,48,128]{3,2,1,0:T(8,128)(2,1)S(1)}, u32[]{:S(2)}, u32[]{:S(2)}) collective-permute-start(bf16[1,8,48,128]{3,2,1,0:T(8,128)(2,1)} %split.3), channel_id=1, source_target_pairs={{0,56},{8,0},{16,8},{24,16},{32,24},{40,32},{48,40},{56,48},{1,57}... | collective-permute-start | bytes 294920 | tf_op jit(solution)/shard_map/along_z/ppermute | solution.py:34
  17.7 0.9 bitcast_dynamic-update-slice_fusion.6
  18.6 1.2 collective-permute-done.6
  19.8 3.2 %collective-permute-start.9 = (bf16[1,8,48,128]{3,2,1,0:T(8,128)(2,1)S(1)}, bf16[1,8,48,128]{3,2,1,0:T(8,128)(2,1)S(1)}, u32[]{:S(2)}, u32[]{:S(2)}) collective-permute-start(bf16[1,8,48,128]{3,2,1,0:T(8,128)(2,1)S(1)} %collective-permute-done.7), channel_id=1, source_target_pairs={{0,56},{8,0},{16,8},{24,16},{32,24},{40,32},{48,40},{56,48},{1,57}... | collective-permute-start | bytes 294920 | tf_op jit(solution)/shard_map/along_z/ppermute | solution.py:34
  23.1 2.5 collective-permute-done.8
  25.6 1.5 collective-permute-done.9
  27.2 3.7 %collective-permute-start.11 = (bf16[1,8,48,128]{3,2,1,0:T(8,128)(2,1)S(1)}, bf16[1,8,48,128]{3,2,1,0:T(8,128)(2,1)S(1)}, u32[]{:S(2)}, u32[]{:S(2)}) collective-permute-start(bf16[1,8,48,128]{3,2,1,0:T(8,128)(2,1)S(1)} %collective-permute-done.9), channel_id=1, source_target_pairs={{0,56},{8,0},{16,8},{24,16},{32,24},{40,32},{48,40},{56,48},{1,57}... | collective-permute-start | bytes 294920 | tf_op jit(solution)/shard_map/along_z/ppermute | solution.py:34
  30.9 4.5 %collective-permute-done.11 = bf16[1,8,48,128]{3,2,1,0:T(8,128)(2,1)S(1)} collective-permute-done((bf16[1,8,48,128]{3,2,1,0:T(8,128)(2,1)S(1)}, bf16[1,8,48,128]{3,2,1,0:T(8,128)(2,1)S(1)}, u32[]{:S(2)}, u32[]{:S(2)}) %collective-permute-start.11) | collective-permute-done | bytes 98336 | tf_op jit(solution)/shard_map/along_z/ppermute | solution.py:34
  35.5 3.7 %collective-permute-start.13 = (bf16[1,4,48,128]{3,2,1,0:T(8,128)(2,1)S(1)}, bf16[1,4,48,128]{3,2,1,0:T(8,128)(2,1)S(1)}, u32[]{:S(2)}, u32[]{:S(2)}) collective-permute-start(bf16[1,4,48,128]{3,2,1,0:T(8,128)(2,1)S(1)} %slice.9), channel_id=1, source_target_pairs={{0,56},{8,0},{16,8},{24,16},{32,24},{40,32},{48,40},{56,48},{1,57}... | collective-permute-start | bytes 147464 | tf_op jit(solution)/shard_map/along_z/ppermute | solution.py:38
  39.3 2.5 collective-permute-done.13
  41.8 3.8 %collective-permute-done.12 = bf16[1,4,48,128]{3,2,1,0:T(8,128)(2,1)S(1)} collective-permute-done((bf16[1,4,48,128]{3,2,1,0:T(8,128)(2,1)S(1)}, bf16[1,4,48,128]{3,2,1,0:T(8,128)(2,1)S(1)}, u32[]{:S(2)}, u32[]{:S(2)}) %collective-permute-start.12) | collective-permute-done | bytes 49184 | tf_op jit(solution)/shard_map/along_z/ppermute | solution.py:37
  46.6 1.4 collective-permute-done.14.refs_1_
  48.0 0.9 copy-done.9
  48.8 3.1 %pick_y.8 = (bf16[32,48,128]{2,1,0:T(8,128)(2,1)S(1)}, bf16[32,48,128]{2,1,0:T(8,128)(2,1)S(1)}, bf16[32,48,128]{2,1,0:T(8,128)(2,1)S(1)}, bf16[32,48,128]{2,1,0:T(8,128)(2,1)}) custom-call(s32[128]{0:T(128)S(1)} %get-tuple-element.56.index_ref, bf16[8,1,8,48,128]{4,3,2,1,0:T(8,128)(2,1)} %copy-done.8, bf16[8,1,8,48,128]{4,3,2,1,0:T(8,128)(2,1)} %copy-done.9), custom_call_target="tpu_custom_call" | custom-call | tf_op jit(solution)/shard_map/along_y/pick_y/pallas_call | solution.py:90
  52.0 3.2 %collective-permute-start.15 = (bf16[32,48,128]{2,1,0:T(8,128)(2,1)}, bf16[32,48,128]{2,1,0:T(8,128)(2,1)S(1)}, u32[]{:S(2)}, u32[]{:S(2)}) collective-permute-start(bf16[32,48,128]{2,1,0:T(8,128)(2,1)} %get-tuple-element.35), channel_id=1, source_target_pairs={{0,192},{64,0},{128,64},{192,128},{1,193},{65,1},{129,65},{193,129... | collective-permute-start | bytes 1179656 | tf_op jit(solution)/shard_map/along_y/ppermute | solution.py:248
  55.7 1.2 collective-permute-start.17
  57.1 12.2 %all-gather.3.cloned.1.call-done = bf16[80,8,48,128]{3,2,1,0:T(8,128)(2,1)} async-done(((bf16[5,8,48,128]{3,2,1,0:T(8,128)(2,1)}), bf16[80,8,48,128]{3,2,1,0:T(8,128)(2,1)}) %all-gather.3.cloned.1.call-update) | async-done | bytes 7864336 | tf_op jit(solution)/shard_map/along_z/all_gather | solution.py:260
  69.3 3.1 %pick_y.6 = (bf16[32,48,128]{2,1,0:T(8,128)(2,1)S(1)}, bf16[32,48,128]{2,1,0:T(8,128)(2,1)S(1)}, bf16[32,48,128]{2,1,0:T(8,128)(2,1)}, bf16[32,48,128]{2,1,0:T(8,128)(2,1)}) custom-call(s32[128]{0:T(128)S(1)} %get-tuple-element.57.index_ref, bf16[16,5,8,48,128]{4,3,2,1,0:T(8,128)(2,1)} %bitcast.70), custom_call_target="tpu_custom_call" | custom-call | tf_op jit(solution)/shard_map/along_y/pick_y/pallas_call | solution.py:90
  72.5 3.0 %collective-permute-start = (bf16[32,48,128]{2,1,0:T(8,128)(2,1)}, bf16[32,48,128]{2,1,0:T(8,128)(2,1)S(1)}, u32[]{:S(2)}, u32[]{:S(2)}) collective-permute-start(bf16[32,48,128]{2,1,0:T(8,128)(2,1)} %get-tuple-element.27), channel_id=1, source_target_pairs={{0,192},{64,0},{128,64},{192,128},{1,193},{65,1},{129,65},{193,129... | collective-permute-start | bytes 1179656 | tf_op jit(solution)/shard_map/along_y/ppermute | solution.py:248
  75.4 0.8 collective-permute-start.1
  76.2 0.9 collective-permute-start.2
  77.1 2.7 %pick_x.8 = bf16[128,48,128]{2,1,0:T(8,128)(2,1)} custom-call(s32[128]{0:T(128)S(1)} %fusion.11.index_ref, bf16[1,1,32,48,128]{4,3,2,1,0:T(8,128)(2,1)S(1)} %bitcast.65, bf16[1,1,32,48,128]{4,3,2,1,0:T(8,128)(2,1)S(1)} %bitcast.67, bf16[1,1,32,48,128]{4,3,2,1,0:T(8,128)(2,1)S(1)} %bitcast.68, bf16[1,1,32,48,128]{4,3,2,1,0:T(8,128)(2,1)S(1)} %bitcast.69), custom_call_target="tpu_custom_call" | custom-call | flops 12000000000 | bytes 36000000 | tf_op jit(solution)/shard_map/along_x/pick_x/pallas_call | solution.py:90
  79.8 4.8 %all-to-all-start.2 = ((bf16[128,48,128]{2,1,0:T(8,128)(2,1)}), bf16[128,48,128]{2,1,0:T(8,128)(2,1)S(1)}, u32[]{:S(2)}, u32[]{:S(2)}) async-start(bf16[128,48,128]{2,1,0:T(8,128)(2,1)} %pick_x.8), calls=%async_computation.2 | async-start | bytes 3145728 | tf_op jit(solution)/shard_map/along_x/all_to_all | solution.py:270
  84.7 3.3 %pick_y.9 = (bf16[32,48,128]{2,1,0:T(8,128)(2,1)S(1)}, bf16[32,48,128]{2,1,0:T(8,128)(2,1)}, bf16[32,48,128]{2,1,0:T(8,128)(2,1)}, bf16[32,48,128]{2,1,0:T(8,128)(2,1)}) custom-call(s32[128]{0:T(128)S(1)} %get-tuple-element.57.index_ref, bf16[16,5,8,48,128]{4,3,2,1,0:T(8,128)(2,1)} %bitcast.71), custom_call_target="tpu_custom_call" | custom-call | tf_op jit(solution)/shard_map/along_y/pick_y/pallas_call | solution.py:90
  87.9 2.4 collective-permute-start.18
  90.4 1.5 collective-permute-start.19
  91.9 1.6 collective-permute-done
  93.5 4.2 %collective-permute-done.2 = bf16[32,48,128]{2,1,0:T(8,128)(2,1)} collective-permute-done((bf16[32,48,128]{2,1,0:T(8,128)(2,1)S(1)}, bf16[32,48,128]{2,1,0:T(8,128)(2,1)}, u32[]{:S(2)}, u32[]{:S(2)}) %collective-permute-start.2) | collective-permute-done | bytes 393248 | tf_op jit(solution)/shard_map/along_y/ppermute | solution.py:248
  97.7 3.5 %pick_x.6 = bf16[128,48,128]{2,1,0:T(8,128)(2,1)} custom-call(s32[128]{0:T(128)S(1)} %fusion.11.index_ref, bf16[1,1,32,48,128]{4,3,2,1,0:T(8,128)(2,1)S(1)} %bitcast.64, bf16[1,1,32,48,128]{4,3,2,1,0:T(8,128)(2,1)S(1)} %bitcast.66, bf16[1,1,32,48,128]{4,3,2,1,0:T(8,128)(2,1)} %bitcast.9.refs_2_, bf16[1,1,32,48,128]{4,3,2,1,0:T(8,128)(2,1)} %bitcast.10.refs_3_), custom_call_target="tpu_custom_call" | custom-call | flops 12000000000 | bytes 36000000 | tf_op jit(solution)/shard_map/along_x/pick_x/pallas_call | solution.py:90
  101.2 2.3 all-to-all-done.2
  103.5 5.0 %all-to-all-start = ((bf16[128,48,128]{2,1,0:T(8,128)(2,1)}), bf16[128,48,128]{2,1,0:T(8,128)(2,1)S(1)}, u32[]{:S(2)}, u32[]{:S(2)}) async-start(bf16[128,48,128]{2,1,0:T(8,128)(2,1)} %pick_x.6), calls=%async_computation | async-start | bytes 3145728 | tf_op jit(solution)/shard_map/along_x/all_to_all | solution.py:270
  108.5 3.3 %pick_y.10 = (bf16[32,48,128]{2,1,0:T(8,128)(2,1)S(1)}, bf16[32,48,128]{2,1,0:T(8,128)(2,1)}, bf16[32,48,128]{2,1,0:T(8,128)(2,1)}, bf16[32,48,128]{2,1,0:T(8,128)(2,1)}) custom-call(s32[128]{0:T(128)S(1)} %get-tuple-element.57.index_ref, bf16[16,5,8,48,128]{4,3,2,1,0:T(8,128)(2,1)} %bitcast.72), custom_call_target="tpu_custom_call" | custom-call | tf_op jit(solution)/shard_map/along_y/pick_y/pallas_call | solution.py:90
  111.8 0.7 copy-done.5
  112.5 2.3 collective-permute-start.21
  114.9 1.5 collective-permute-start.22
  116.4 3.3 %pick_x.9 = bf16[128,48,128]{2,1,0:T(8,128)(2,1)} custom-call(s32[128]{0:T(128)S(1)} %fusion.11.index_ref, bf16[1,1,32,48,128]{4,3,2,1,0:T(8,128)(2,1)S(1)} %bitcast.62, bf16[1,1,32,48,128]{4,3,2,1,0:T(8,128)(2,1)} %bitcast.31.refs_1_, bf16[1,1,32,48,128]{4,3,2,1,0:T(8,128)(2,1)} %bitcast.32.refs_2_, bf16[1,1,32,48,128]{4,3,2,1,0:T(8,128)(2,1)} %bitcast.33.refs_3_), custom_call_target="tpu_custom_call" | custom-call | flops 12000000000 | bytes 36000000 | tf_op jit(solution)/shard_map/along_x/pick_x/pallas_call | solution.py:90
  119.8 6.7 %all-to-all-done = bf16[128,48,128]{2,1,0:T(8,128)(2,1)S(1)} async-done(((bf16[128,48,128]{2,1,0:T(8,128)(2,1)}), bf16[128,48,128]{2,1,0:T(8,128)(2,1)S(1)}, u32[]{:S(2)}, u32[]{:S(2)}) %all-to-all-start) | async-done | bytes 1572896 | tf_op jit(solution)/shard_map/along_x/all_to_all | solution.py:270
  126.5 5.8 %all-to-all-start.3 = ((bf16[128,48,128]{2,1,0:T(8,128)(2,1)}), bf16[128,48,128]{2,1,0:T(8,128)(2,1)}, u32[]{:S(2)}, u32[]{:S(2)}) async-start(bf16[128,48,128]{2,1,0:T(8,128)(2,1)} %pick_x.9), calls=%async_computation.3 | async-start | bytes 3145728 | tf_op jit(solution)/shard_map/along_x/all_to_all | solution.py:270
  132.3 3.3 %pick_y.11 = (bf16[32,48,128]{2,1,0:T(8,128)(2,1)S(1)}, bf16[32,48,128]{2,1,0:T(8,128)(2,1)}, bf16[32,48,128]{2,1,0:T(8,128)(2,1)}, bf16[32,48,128]{2,1,0:T(8,128)(2,1)}) custom-call(s32[128]{0:T(128)S(1)} %get-tuple-element.57.index_ref, bf16[16,5,8,48,128]{4,3,2,1,0:T(8,128)(2,1)} %bitcast.73), custom_call_target="tpu_custom_call" | custom-call | tf_op jit(solution)/shard_map/along_y/pick_y/pallas_call | solution.py:90
  135.6 0.7 copy-done.3
  136.4 2.3 collective-permute-start.24
  138.7 1.4 collective-permute-start.25
  140.2 3.4 %pick_x.10 = bf16[128,48,128]{2,1,0:T(8,128)(2,1)} custom-call(s32[128]{0:T(128)S(1)} %fusion.11.index_ref, bf16[1,1,32,48,128]{4,3,2,1,0:T(8,128)(2,1)S(1)} %bitcast.63, bf16[1,1,32,48,128]{4,3,2,1,0:T(8,128)(2,1)} %bitcast.36.refs_1_, bf16[1,1,32,48,128]{4,3,2,1,0:T(8,128)(2,1)} %bitcast.37.refs_2_, bf16[1,1,32,48,128]{4,3,2,1,0:T(8,128)(2,1)} %bitcast.38.refs_3_), custom_call_target="tpu_custom_call" | custom-call | flops 12000000000 | bytes 36000000 | tf_op jit(solution)/shard_map/along_x/pick_x/pallas_call | solution.py:90
  143.6 5.9 %all-to-all-done.3 = bf16[128,48,128]{2,1,0:T(8,128)(2,1)} async-done(((bf16[128,48,128]{2,1,0:T(8,128)(2,1)}), bf16[128,48,128]{2,1,0:T(8,128)(2,1)}, u32[]{:S(2)}, u32[]{:S(2)}) %all-to-all-start.3) | async-done | bytes 1572896 | tf_op jit(solution)/shard_map/along_x/all_to_all | solution.py:270
  149.6 5.8 %all-to-all-start.4 = ((bf16[128,48,128]{2,1,0:T(8,128)(2,1)}), bf16[128,48,128]{2,1,0:T(8,128)(2,1)}, u32[]{:S(2)}, u32[]{:S(2)}) async-start(bf16[128,48,128]{2,1,0:T(8,128)(2,1)} %pick_x.10), calls=%async_computation.4 | async-start | bytes 3145728 | tf_op jit(solution)/shard_map/along_x/all_to_all | solution.py:270
  155.3 3.3 %pick_y.7 = (bf16[32,48,128]{2,1,0:T(8,128)(2,1)S(1)}, bf16[32,48,128]{2,1,0:T(8,128)(2,1)}, bf16[32,48,128]{2,1,0:T(8,128)(2,1)}, bf16[32,48,128]{2,1,0:T(8,128)(2,1)}) custom-call(s32[128]{0:T(128)S(1)} %get-tuple-element.57.index_ref, bf16[16,5,8,48,128]{4,3,2,1,0:T(8,128)(2,1)} %bitcast.74), custom_call_target="tpu_custom_call" | custom-call | tf_op jit(solution)/shard_map/along_y/pick_y/pallas_call | solution.py:90
  158.6 2.4 collective-permute-start.3
  161.0 1.2 collective-permute-start.4
  162.5 3.4 %pick_x.11 = bf16[128,48,128]{2,1,0:T(8,128)(2,1)} custom-call(s32[128]{0:T(128)S(1)} %fusion.11.index_ref, bf16[1,1,32,48,128]{4,3,2,1,0:T(8,128)(2,1)S(1)} %bitcast.61, bf16[1,1,32,48,128]{4,3,2,1,0:T(8,128)(2,1)} %bitcast.41.refs_1_, bf16[1,1,32,48,128]{4,3,2,1,0:T(8,128)(2,1)} %bitcast.42.refs_2_, bf16[1,1,32,48,128]{4,3,2,1,0:T(8,128)(2,1)} %bitcast.43.refs_3_), custom_call_target="tpu_custom_call" | custom-call | flops 12000000000 | bytes 36000000 | tf_op jit(solution)/shard_map/along_x/pick_x/pallas_call | solution.py:90
  165.9 5.8 %all-to-all-done.4 = bf16[128,48,128]{2,1,0:T(8,128)(2,1)} async-done(((bf16[128,48,128]{2,1,0:T(8,128)(2,1)}), bf16[128,48,128]{2,1,0:T(8,128)(2,1)}, u32[]{:S(2)}, u32[]{:S(2)}) %all-to-all-start.4) | async-done | bytes 1572896 | tf_op jit(solution)/shard_map/along_x/all_to_all | solution.py:270
  171.7 5.8 %all-to-all-start.5 = ((bf16[128,48,128]{2,1,0:T(8,128)(2,1)}), bf16[128,48,128]{2,1,0:T(8,128)(2,1)}, u32[]{:S(2)}, u32[]{:S(2)}) async-start(bf16[128,48,128]{2,1,0:T(8,128)(2,1)} %pick_x.11), calls=%async_computation.5 | async-start | bytes 3145728 | tf_op jit(solution)/shard_map/along_x/all_to_all | solution.py:270
  177.5 0.8 dynamic_slice.24
  178.3 3.4 %pick_x.7 = bf16[128,48,128]{2,1,0:T(8,128)(2,1)} custom-call(s32[128]{0:T(128)S(1)} %fusion.11.index_ref, bf16[1,1,32,48,128]{4,3,2,1,0:T(8,128)(2,1)S(1)} %bitcast.60, bf16[1,1,32,48,128]{4,3,2,1,0:T(8,128)(2,1)} %bitcast.13.refs_1_, bf16[1,1,32,48,128]{4,3,2,1,0:T(8,128)(2,1)} %bitcast.14.refs_2_, bf16[1,1,32,48,128]{4,3,2,1,0:T(8,128)(2,1)} %bitcast.15.refs_3_), custom_call_target="tpu_custom_call" | custom-call | flops 12000000000 | bytes 36000000 | tf_op jit(solution)/shard_map/along_x/pick_x/pallas_call | solution.py:90
  181.8 11.2 %all-to-all-done.5 = bf16[128,48,128]{2,1,0:T(8,128)(2,1)} async-done(((bf16[128,48,128]{2,1,0:T(8,128)(2,1)}), bf16[128,48,128]{2,1,0:T(8,128)(2,1)}, u32[]{:S(2)}, u32[]{:S(2)}) %all-to-all-start.5) | async-done | bytes 1572896 | tf_op jit(solution)/shard_map/along_x/all_to_all | solution.py:270
  193.0 5.8 %all-to-all-start.1 = ((bf16[128,48,128]{2,1,0:T(8,128)(2,1)}), bf16[128,48,128]{2,1,0:T(8,128)(2,1)}, u32[]{:S(2)}, u32[]{:S(2)}) async-start(bf16[128,48,128]{2,1,0:T(8,128)(2,1)} %pick_x.7), calls=%async_computation.1 | async-start | bytes 3145728 | tf_op jit(solution)/shard_map/along_x/all_to_all | solution.py:270
  199.0 12.4 %couple.2.rest_2_ = f32[8,384,384]{2,1,0:T(8,128)} custom-call(s32[32]{0:T(128)S(1)} %and_select_fusion.4.target, f32[32]{0:T(128)S(1)} %copy-done.2, bf16[32,384,384]{2,1,0:T(8,128)(2,1)} %s_ref.3, bf16[4,32,48,128]{3,2,1,0:T(8,128)(2,1)S(1)} %bitcast.59, bf16[4,32,48,128]{3,2,1,0:T(8,128)(2,1)} %bitcast.34.rest_1_, ...), custom_call_target="tpu_custom_call" | custom-call | flops 9663676416 | bytes 14155776 | tf_op jit(solution)/shard_map/couple/couple/pallas_call | solution.py:281
  211.3 1.7 all-to-all-done.1
  213.0 12.2 %couple.3 = bf16[4,8,96,384]{3,2,1,0:T(8,128)(2,1)} custom-call(s32[32]{0:T(128)S(1)} %and_select_fusion.4.target, f32[32]{0:T(128)S(1)} %copy-done.2, bf16[32,384,384]{2,1,0:T(8,128)(2,1)} %s_ref.3, bf16[4,32,48,128]{3,2,1,0:T(8,128)(2,1)S(1)} %bitcast.58, bf16[4,32,48,128]{3,2,1,0:T(8,128)(2,1)} %bitcast.16.rest_1_, f32[8,384,384]{2,1,0:T(8,128)} %couple.2.rest_2_), custom_call_target="tpu_custom_call" | custom-call | flops 4831838208 | bytes 14155776 | tf_op jit(solution)/shard_map/couple/couple/pallas_call | solution.py:281
  225.2 5.1 %all-to-all-start.6 = ((bf16[4,8,96,384]{3,2,1,0:T(8,128)(2,1)}), bf16[4,8,96,384]{3,2,1,0:T(8,128)(2,1)S(1)}, u32[]{:S(2)}, u32[]{:S(2)}) async-start(bf16[4,8,96,384]{3,2,1,0:T(8,128)(2,1)} %couple.3), calls=%async_computation.6 | async-start | bytes 4718592 | tf_op jit(solution)/shard_map/sum_x/all_to_all | solution.py:283
  230.4 21.3 %all-to-all-done.6 = bf16[4,8,96,384]{3,2,1,0:T(8,128)(2,1)S(1)} async-done(((bf16[4,8,96,384]{3,2,1,0:T(8,128)(2,1)}), bf16[4,8,96,384]{3,2,1,0:T(8,128)(2,1)S(1)}, u32[]{:S(2)}, u32[]{:S(2)}) %all-to-all-start.6) | async-done | bytes 2359328 | tf_op jit(solution)/shard_map/sum_x/all_to_all | solution.py:283
  252.7 1.9 convert_subtract_fusion
  (92 shorter events, 4.4 us)
Async XLA Ops:
  7.2 9.7 %copy-start = (s32[8192]{0:T(1024)S(1)}, s32[8192]{0:T(1024)}, u32[]{:S(2)}) copy-start(s32[8192]{0:T(1024)} %param.15) | copy-start | bytes 98308
  7.2 9.7 %copy-start.14 = (s32[8]{0:T(128)S(1)}, s32[8]{0:T(128)}, u32[]{:S(2)}) copy-start(s32[8]{0:T(128)} %constant.177.clone) | copy-start | bytes 100
  7.2 9.9 %copy-start.12 = (s32[512]{0:T(512)S(1)}, s32[512]{0:T(512)}, u32[]{:S(2)}) copy-start(s32[512]{0:T(512)} %param.14) | copy-start | bytes 6148
  7.2 62.1 %all-gather.3.cloned.1.call-start = ((), (), s32[]{:S(2)}) async-start(), calls=%async_computation.7 | async-start | bytes 8355840 | tf_op jit(solution)/shard_map/along_z/all_gather | solution.py:260
  11.0 8.9 %collective-permute-start.6 = (bf16[1,8,48,128]{3,2,1,0:T(8,128)(2,1)}, bf16[1,8,48,128]{3,2,1,0:T(8,128)(2,1)S(1)}, u32[]{:S(2)}, u32[]{:S(2)}) collective-permute-start(bf16[1,8,48,128]{3,2,1,0:T(8,128)(2,1)} %split.3), channel_id=1, source_target_pairs={{0,8},{8,16},{16,24},{24,32},{32,40},{40,48},{48,56},{56,0},{1,9},... | collective-permute-start | bytes 294920 | tf_op jit(solution)/shard_map/along_z/ppermute | solution.py:33
  12.9 6.9 %collective-permute-start.7 = (bf16[1,8,48,128]{3,2,1,0:T(8,128)(2,1)}, bf16[1,8,48,128]{3,2,1,0:T(8,128)(2,1)S(1)}, u32[]{:S(2)}, u32[]{:S(2)}) collective-permute-start(bf16[1,8,48,128]{3,2,1,0:T(8,128)(2,1)} %split.3), channel_id=1, source_target_pairs={{0,56},{8,0},{16,8},{24,16},{32,24},{40,32},{48,40},{56,48},{1,57}... | collective-permute-start | bytes 294920 | tf_op jit(solution)/shard_map/along_z/ppermute | solution.py:34
  19.8 5.8 %collective-permute-start.8 = (bf16[1,8,48,128]{3,2,1,0:T(8,128)(2,1)S(1)}, bf16[1,8,48,128]{3,2,1,0:T(8,128)(2,1)S(1)}, u32[]{:S(2)}, u32[]{:S(2)}) collective-permute-start(bf16[1,8,48,128]{3,2,1,0:T(8,128)(2,1)S(1)} %collective-permute-done.6), channel_id=1, source_target_pairs={{0,8},{8,16},{16,24},{24,32},{32,40},{40,48},{48,56},{56,0},{1,9},... | collective-permute-start | bytes 294920 | tf_op jit(solution)/shard_map/along_z/ppermute | solution.py:33
  19.8 7.4 %collective-permute-start.9 = (bf16[1,8,48,128]{3,2,1,0:T(8,128)(2,1)S(1)}, bf16[1,8,48,128]{3,2,1,0:T(8,128)(2,1)S(1)}, u32[]{:S(2)}, u32[]{:S(2)}) collective-permute-start(bf16[1,8,48,128]{3,2,1,0:T(8,128)(2,1)S(1)} %collective-permute-done.7), channel_id=1, source_target_pairs={{0,56},{8,0},{16,8},{24,16},{32,24},{40,32},{48,40},{56,48},{1,57}... | collective-permute-start | bytes 294920 | tf_op jit(solution)/shard_map/along_z/ppermute | solution.py:34
  25.6 13.5 %collective-permute-start.10 = (bf16[1,8,48,128]{3,2,1,0:T(8,128)(2,1)S(1)}, bf16[1,8,48,128]{3,2,1,0:T(8,128)(2,1)S(1)}, u32[]{:S(2)}, u32[]{:S(2)}) collective-permute-start(bf16[1,8,48,128]{3,2,1,0:T(8,128)(2,1)S(1)} %collective-permute-done.8), channel_id=1, source_target_pairs={{0,8},{8,16},{16,24},{24,32},{32,40},{40,48},{48,56},{56,0},{1,9},... | collective-permute-start | bytes 294920 | tf_op jit(solution)/shard_map/along_z/ppermute | solution.py:33
  27.2 8.3 %collective-permute-start.11 = (bf16[1,8,48,128]{3,2,1,0:T(8,128)(2,1)S(1)}, bf16[1,8,48,128]{3,2,1,0:T(8,128)(2,1)S(1)}, u32[]{:S(2)}, u32[]{:S(2)}) collective-permute-start(bf16[1,8,48,128]{3,2,1,0:T(8,128)(2,1)S(1)} %collective-permute-done.9), channel_id=1, source_target_pairs={{0,56},{8,0},{16,8},{24,16},{32,24},{40,32},{48,40},{56,48},{1,57}... | collective-permute-start | bytes 294920 | tf_op jit(solution)/shard_map/along_z/ppermute | solution.py:34
  35.5 6.3 %collective-permute-start.13 = (bf16[1,4,48,128]{3,2,1,0:T(8,128)(2,1)S(1)}, bf16[1,4,48,128]{3,2,1,0:T(8,128)(2,1)S(1)}, u32[]{:S(2)}, u32[]{:S(2)}) collective-permute-start(bf16[1,4,48,128]{3,2,1,0:T(8,128)(2,1)S(1)} %slice.9), channel_id=1, source_target_pairs={{0,56},{8,0},{16,8},{24,16},{32,24},{40,32},{48,40},{56,48},{1,57}... | collective-permute-start | bytes 147464 | tf_op jit(solution)/shard_map/along_z/ppermute | solution.py:38
  39.2 6.4 %collective-permute-start.12 = (bf16[1,4,48,128]{3,2,1,0:T(8,128)(2,1)S(1)}, bf16[1,4,48,128]{3,2,1,0:T(8,128)(2,1)S(1)}, u32[]{:S(2)}, u32[]{:S(2)}) collective-permute-start(bf16[1,4,48,128]{3,2,1,0:T(8,128)(2,1)S(1)} %slice.8), channel_id=1, source_target_pairs={{0,8},{8,16},{16,24},{24,32},{32,40},{40,48},{48,56},{56,0},{1,9},... | collective-permute-start | bytes 147464 | tf_op jit(solution)/shard_map/along_z/ppermute | solution.py:37
  45.6 3.3 %copy-start.8 = (bf16[8,1,8,48,128]{4,3,2,1,0:T(8,128)(2,1)}, bf16[8,1,8,48,128]{4,3,2,1,0:T(8,128)(2,1)S(1)}, u32[]{:S(2)}) copy-start(bf16[8,1,8,48,128]{4,3,2,1,0:T(8,128)(2,1)S(1)} %fusion.2.refs_0_) | copy-start | bytes 2359300
  45.6 2.4 collective-permute-start.14
  48.0 0.9 copy-start.9
  52.0 24.2 %collective-permute-start.15 = (bf16[32,48,128]{2,1,0:T(8,128)(2,1)}, bf16[32,48,128]{2,1,0:T(8,128)(2,1)S(1)}, u32[]{:S(2)}, u32[]{:S(2)}) collective-permute-start(bf16[32,48,128]{2,1,0:T(8,128)(2,1)} %get-tuple-element.35), channel_id=1, source_target_pairs={{0,192},{64,0},{128,64},{192,128},{1,193},{65,1},{129,65},{193,129... | collective-permute-start | bytes 1179656 | tf_op jit(solution)/shard_map/along_y/ppermute | solution.py:248
  55.2 21.9 %collective-permute-start.16 = (bf16[32,48,128]{2,1,0:T(8,128)(2,1)S(1)}, bf16[32,48,128]{2,1,0:T(8,128)(2,1)S(1)}, u32[]{:S(2)}, u32[]{:S(2)}) collective-permute-start(bf16[32,48,128]{2,1,0:T(8,128)(2,1)S(1)} %get-tuple-element.36), channel_id=1, source_target_pairs={{0,128},{64,192},{128,0},{192,64},{1,129},{65,193},{129,1},{193,65... | collective-permute-start | bytes 1179656 | tf_op jit(solution)/shard_map/along_y/ppermute | solution.py:248
  55.7 21.5 %collective-permute-start.17 = (bf16[32,48,128]{2,1,0:T(8,128)(2,1)S(1)}, bf16[32,48,128]{2,1,0:T(8,128)(2,1)S(1)}, u32[]{:S(2)}, u32[]{:S(2)}) collective-permute-start(bf16[32,48,128]{2,1,0:T(8,128)(2,1)S(1)} %get-tuple-element.37), channel_id=1, source_target_pairs={{0,64},{64,128},{128,192},{192,0},{1,65},{65,129},{129,193},{193,1... | collective-permute-start | bytes 1179656 | tf_op jit(solution)/shard_map/along_y/ppermute | solution.py:248
  72.5 21.0 %collective-permute-start = (bf16[32,48,128]{2,1,0:T(8,128)(2,1)}, bf16[32,48,128]{2,1,0:T(8,128)(2,1)S(1)}, u32[]{:S(2)}, u32[]{:S(2)}) collective-permute-start(bf16[32,48,128]{2,1,0:T(8,128)(2,1)} %get-tuple-element.27), channel_id=1, source_target_pairs={{0,192},{64,0},{128,64},{192,128},{1,193},{65,1},{129,65},{193,129... | collective-permute-start | bytes 1179656 | tf_op jit(solution)/shard_map/along_y/ppermute | solution.py:248
  75.4 18.1 %collective-permute-start.1 = (bf16[32,48,128]{2,1,0:T(8,128)(2,1)}, bf16[32,48,128]{2,1,0:T(8,128)(2,1)}, u32[]{:S(2)}, u32[]{:S(2)}) collective-permute-start(bf16[32,48,128]{2,1,0:T(8,128)(2,1)} %get-tuple-element.28), channel_id=1, source_target_pairs={{0,128},{64,192},{128,0},{192,64},{1,129},{65,193},{129,1},{193,65... | collective-permute-start | bytes 1179656 | tf_op jit(solution)/shard_map/along_y/ppermute | solution.py:248
  76.2 21.5 %collective-permute-start.2 = (bf16[32,48,128]{2,1,0:T(8,128)(2,1)S(1)}, bf16[32,48,128]{2,1,0:T(8,128)(2,1)}, u32[]{:S(2)}, u32[]{:S(2)}) collective-permute-start(bf16[32,48,128]{2,1,0:T(8,128)(2,1)S(1)} %get-tuple-element.29), channel_id=1, source_target_pairs={{0,64},{64,128},{128,192},{192,0},{1,65},{65,129},{129,193},{193,1... | collective-permute-start | bytes 1179656 | tf_op jit(solution)/shard_map/along_y/ppermute | solution.py:248
  79.8 23.6 %all-to-all-start.2 = ((bf16[128,48,128]{2,1,0:T(8,128)(2,1)}), bf16[128,48,128]{2,1,0:T(8,128)(2,1)S(1)}, u32[]{:S(2)}, u32[]{:S(2)}) async-start(bf16[128,48,128]{2,1,0:T(8,128)(2,1)} %pick_x.8), calls=%async_computation.2 | async-start | bytes 3145728 | tf_op jit(solution)/shard_map/along_x/all_to_all | solution.py:270
  87.9 28.5 %collective-permute-start.18 = (bf16[32,48,128]{2,1,0:T(8,128)(2,1)}, bf16[32,48,128]{2,1,0:T(8,128)(2,1)}, u32[]{:S(2)}, u32[]{:S(2)}) collective-permute-start(bf16[32,48,128]{2,1,0:T(8,128)(2,1)} %get-tuple-element.39), channel_id=1, source_target_pairs={{0,192},{64,0},{128,64},{192,128},{1,193},{65,1},{129,65},{193,129... | collective-permute-start | bytes 1179656 | tf_op jit(solution)/shard_map/along_y/ppermute | solution.py:248
  90.4 26.1 %collective-permute-start.19 = (bf16[32,48,128]{2,1,0:T(8,128)(2,1)}, bf16[32,48,128]{2,1,0:T(8,128)(2,1)}, u32[]{:S(2)}, u32[]{:S(2)}) collective-permute-start(bf16[32,48,128]{2,1,0:T(8,128)(2,1)} %get-tuple-element.40), channel_id=1, source_target_pairs={{0,128},{64,192},{128,0},{192,64},{1,129},{65,193},{129,1},{193,65... | collective-permute-start | bytes 1179656 | tf_op jit(solution)/shard_map/along_y/ppermute | solution.py:248
  93.5 22.9 %collective-permute-start.20 = (bf16[32,48,128]{2,1,0:T(8,128)(2,1)}, bf16[32,48,128]{2,1,0:T(8,128)(2,1)}, u32[]{:S(2)}, u32[]{:S(2)}) collective-permute-start(bf16[32,48,128]{2,1,0:T(8,128)(2,1)} %get-tuple-element.41), channel_id=1, source_target_pairs={{0,64},{64,128},{128,192},{192,0},{1,65},{65,129},{129,193},{193,1... | collective-permute-start | bytes 1179656 | tf_op jit(solution)/shard_map/along_y/ppermute | solution.py:248
  103.5 23.0 %all-to-all-start = ((bf16[128,48,128]{2,1,0:T(8,128)(2,1)}), bf16[128,48,128]{2,1,0:T(8,128)(2,1)S(1)}, u32[]{:S(2)}, u32[]{:S(2)}) async-start(bf16[128,48,128]{2,1,0:T(8,128)(2,1)} %pick_x.6), calls=%async_computation | async-start | bytes 3145728 | tf_op jit(solution)/shard_map/along_x/all_to_all | solution.py:270
  111.8 0.8 copy-start.5
  112.5 27.6 %collective-permute-start.21 = (bf16[32,48,128]{2,1,0:T(8,128)(2,1)}, bf16[32,48,128]{2,1,0:T(8,128)(2,1)}, u32[]{:S(2)}, u32[]{:S(2)}) collective-permute-start(bf16[32,48,128]{2,1,0:T(8,128)(2,1)} %get-tuple-element.43), channel_id=1, source_target_pairs={{0,192},{64,0},{128,64},{192,128},{1,193},{65,1},{129,65},{193,129... | collective-permute-start | bytes 1179656 | tf_op jit(solution)/shard_map/along_y/ppermute | solution.py:248
  114.9 25.3 %collective-permute-start.22 = (bf16[32,48,128]{2,1,0:T(8,128)(2,1)}, bf16[32,48,128]{2,1,0:T(8,128)(2,1)}, u32[]{:S(2)}, u32[]{:S(2)}) collective-permute-start(bf16[32,48,128]{2,1,0:T(8,128)(2,1)} %get-tuple-element.44), channel_id=1, source_target_pairs={{0,128},{64,192},{128,0},{192,64},{1,129},{65,193},{129,1},{193,65... | collective-permute-start | bytes 1179656 | tf_op jit(solution)/shard_map/along_y/ppermute | solution.py:248
  116.4 23.7 %collective-permute-start.23 = (bf16[32,48,128]{2,1,0:T(8,128)(2,1)}, bf16[32,48,128]{2,1,0:T(8,128)(2,1)}, u32[]{:S(2)}, u32[]{:S(2)}) collective-permute-start(bf16[32,48,128]{2,1,0:T(8,128)(2,1)} %get-tuple-element.45), channel_id=1, source_target_pairs={{0,64},{64,128},{128,192},{192,0},{1,65},{65,129},{129,193},{193,1... | collective-permute-start | bytes 1179656 | tf_op jit(solution)/shard_map/along_y/ppermute | solution.py:248
  126.5 23.1 %all-to-all-start.3 = ((bf16[128,48,128]{2,1,0:T(8,128)(2,1)}), bf16[128,48,128]{2,1,0:T(8,128)(2,1)}, u32[]{:S(2)}, u32[]{:S(2)}) async-start(bf16[128,48,128]{2,1,0:T(8,128)(2,1)} %pick_x.9), calls=%async_computation.3 | async-start | bytes 3145728 | tf_op jit(solution)/shard_map/along_x/all_to_all | solution.py:270
  132.3 7.9 %copy-start.6 = (bf16[32,48,128]{2,1,0:T(8,128)(2,1)S(1)}, bf16[32,48,128]{2,1,0:T(8,128)(2,1)}, u32[]{:S(2)}) copy-start(bf16[32,48,128]{2,1,0:T(8,128)(2,1)} %copy-done.5) | copy-start | bytes 1179652
  135.6 0.8 copy-start.3
  136.4 25.9 %collective-permute-start.24 = (bf16[32,48,128]{2,1,0:T(8,128)(2,1)}, bf16[32,48,128]{2,1,0:T(8,128)(2,1)}, u32[]{:S(2)}, u32[]{:S(2)}) collective-permute-start(bf16[32,48,128]{2,1,0:T(8,128)(2,1)} %get-tuple-element.47), channel_id=1, source_target_pairs={{0,192},{64,0},{128,64},{192,128},{1,193},{65,1},{129,65},{193,129... | collective-permute-start | bytes 1179656 | tf_op jit(solution)/shard_map/along_y/ppermute | solution.py:248
  138.7 23.8 %collective-permute-start.25 = (bf16[32,48,128]{2,1,0:T(8,128)(2,1)}, bf16[32,48,128]{2,1,0:T(8,128)(2,1)}, u32[]{:S(2)}, u32[]{:S(2)}) collective-permute-start(bf16[32,48,128]{2,1,0:T(8,128)(2,1)} %get-tuple-element.48), channel_id=1, source_target_pairs={{0,128},{64,192},{128,0},{192,64},{1,129},{65,193},{129,1},{193,65... | collective-permute-start | bytes 1179656 | tf_op jit(solution)/shard_map/along_y/ppermute | solution.py:248
  140.1 22.4 %collective-permute-start.26 = (bf16[32,48,128]{2,1,0:T(8,128)(2,1)}, bf16[32,48,128]{2,1,0:T(8,128)(2,1)}, u32[]{:S(2)}, u32[]{:S(2)}) collective-permute-start(bf16[32,48,128]{2,1,0:T(8,128)(2,1)} %get-tuple-element.49), channel_id=1, source_target_pairs={{0,64},{64,128},{128,192},{192,0},{1,65},{65,129},{129,193},{193,1... | collective-permute-start | bytes 1179656 | tf_op jit(solution)/shard_map/along_y/ppermute | solution.py:248
  149.6 22.1 %all-to-all-start.4 = ((bf16[128,48,128]{2,1,0:T(8,128)(2,1)}), bf16[128,48,128]{2,1,0:T(8,128)(2,1)}, u32[]{:S(2)}, u32[]{:S(2)}) async-start(bf16[128,48,128]{2,1,0:T(8,128)(2,1)} %pick_x.10), calls=%async_computation.4 | async-start | bytes 3145728 | tf_op jit(solution)/shard_map/along_x/all_to_all | solution.py:270
  155.3 7.2 %copy-start.4 = (bf16[32,48,128]{2,1,0:T(8,128)(2,1)S(1)}, bf16[32,48,128]{2,1,0:T(8,128)(2,1)}, u32[]{:S(2)}) copy-start(bf16[32,48,128]{2,1,0:T(8,128)(2,1)} %copy-done.3) | copy-start | bytes 1179652
  158.6 19.6 %collective-permute-start.3 = (bf16[32,48,128]{2,1,0:T(8,128)(2,1)}, bf16[32,48,128]{2,1,0:T(8,128)(2,1)}, u32[]{:S(2)}, u32[]{:S(2)}) collective-permute-start(bf16[32,48,128]{2,1,0:T(8,128)(2,1)} %get-tuple-element.31), channel_id=1, source_target_pairs={{0,192},{64,0},{128,64},{192,128},{1,193},{65,1},{129,65},{193,129... | collective-permute-start | bytes 1179656 | tf_op jit(solution)/shard_map/along_y/ppermute | solution.py:248
  161.0 17.2 %collective-permute-start.4 = (bf16[32,48,128]{2,1,0:T(8,128)(2,1)}, bf16[32,48,128]{2,1,0:T(8,128)(2,1)}, u32[]{:S(2)}, u32[]{:S(2)}) collective-permute-start(bf16[32,48,128]{2,1,0:T(8,128)(2,1)} %get-tuple-element.32), channel_id=1, source_target_pairs={{0,128},{64,192},{128,0},{192,64},{1,129},{65,193},{129,1},{193,65... | collective-permute-start | bytes 1179656 | tf_op jit(solution)/shard_map/along_y/ppermute | solution.py:248
  162.3 16.1 %collective-permute-start.5 = (bf16[32,48,128]{2,1,0:T(8,128)(2,1)}, bf16[32,48,128]{2,1,0:T(8,128)(2,1)}, u32[]{:S(2)}, u32[]{:S(2)}) collective-permute-start(bf16[32,48,128]{2,1,0:T(8,128)(2,1)} %get-tuple-element.33), channel_id=1, source_target_pairs={{0,64},{64,128},{128,192},{192,0},{1,65},{65,129},{129,193},{193,1... | collective-permute-start | bytes 1179656 | tf_op jit(solution)/shard_map/along_y/ppermute | solution.py:248
  171.7 21.3 %all-to-all-start.5 = ((bf16[128,48,128]{2,1,0:T(8,128)(2,1)}), bf16[128,48,128]{2,1,0:T(8,128)(2,1)}, u32[]{:S(2)}, u32[]{:S(2)}) async-start(bf16[128,48,128]{2,1,0:T(8,128)(2,1)} %pick_x.11), calls=%async_computation.5 | async-start | bytes 3145728 | tf_op jit(solution)/shard_map/along_x/all_to_all | solution.py:270
  181.8 17.2 %copy-start.2 = (f32[32]{0:T(128)S(1)}, f32[32]{0:T(128)}, u32[]{:S(2)}) copy-start(f32[32]{0:T(128)} %fock.3) | copy-start | bytes 388
  193.0 20.0 %all-to-all-start.1 = ((bf16[128,48,128]{2,1,0:T(8,128)(2,1)}), bf16[128,48,128]{2,1,0:T(8,128)(2,1)}, u32[]{:S(2)}, u32[]{:S(2)}) async-start(bf16[128,48,128]{2,1,0:T(8,128)(2,1)} %pick_x.7), calls=%async_computation.1 | async-start | bytes 3145728 | tf_op jit(solution)/shard_map/along_x/all_to_all | solution.py:270
  225.2 5.1 %copy-start.11 = (f32[8,384]{1,0:T(8,128)S(1)}, f32[8,384]{1,0:T(8,128)}, u32[]{:S(2)}) copy-start(f32[8,384]{1,0:T(8,128)} %param.12) | copy-start | bytes 36868
  225.2 26.4 %all-to-all-start.6 = ((bf16[4,8,96,384]{3,2,1,0:T(8,128)(2,1)}), bf16[4,8,96,384]{3,2,1,0:T(8,128)(2,1)S(1)}, u32[]{:S(2)}, u32[]{:S(2)}) async-start(bf16[4,8,96,384]{3,2,1,0:T(8,128)(2,1)} %couple.3), calls=%async_computation.6 | async-start | bytes 4718592 | tf_op jit(solution)/shard_map/sum_x/all_to_all | solution.py:283
  230.4 21.6 %copy-start.7 = (bf16[8,96,384]{2,1,0:T(8,128)(2,1)S(1)}, bf16[8,96,384]{2,1,0:T(8,128)(2,1)}, u32[]{:S(2)}) copy-start(bf16[8,96,384]{2,1,0:T(8,128)(2,1)} %in_ref.3) | copy-start | bytes 1769476
  230.4 21.6 %copy-start.13 = (f32[8]{0:T(128)S(1)}, f32[8]{0:T(128)}, u32[]{:S(2)}) copy-start(f32[8]{0:T(128)} %param.13) | copy-start | bytes 100
  251.7 1.1 copy-start.10
  251.7 3.0 %copy-start.1 = (s32[8192]{0:T(1024)S(1)}, s32[8192]{0:T(1024)}, u32[]{:S(2)}) copy-start(s32[8192]{0:T(1024)} %param.15) | copy-start | bytes 98308
Sparse Core Ops, SparseCore 0:
  9.9 59.4 all-gather.2

commit v3 on v2

--- a/solution.py
+++ b/solution.py
@@ -25,23 +25,32 @@
 
 def ring_gather(block):
     count = lax.axis_size("z")
-    up = [(i, (i + 1) % count) for i in range(count)]
-    down = [(i, (i - 1) % count) for i in range(count)]
-    parts = [block]
-    above = below = block
-    for _ in range(count // 2 - 1):
-        above = lax.ppermute(above, "z", up)
-        below = lax.ppermute(below, "z", down)
-        parts += [above, below]
+
+    def shift(array, step):
+        return lax.ppermute(array, "z", [(i, (i + step) % count) for i in range(count)])
+
+    one_above, one_below = shift(block, 1), shift(block, -1)
+    two_above, two_below = shift(block, 2), shift(block, -2)
+    three_above, three_below = shift(two_above, 1), shift(two_below, -1)
     half = block.shape[1] // 2
-    above = lax.ppermute(above[:, :half], "z", up)
-    below = lax.ppermute(below[:, half:], "z", down)
-    parts.append(jnp.concatenate([above, below], axis=1))
-    return jnp.stack(parts)
+    across = [shift(two_above[:, :half], 2), shift(two_below[:, half:], -2)]
+    parts = [block, one_above, one_below, two_above, two_below, three_above, three_below]
+    return jnp.stack(parts + [jnp.concatenate(across, axis=1)])
 
 
 def split(amplitude, piece, members):
     pairs, _, _ = amplitude.shape
+
+    if len(members) == 1:
+        j, r = members[0]
+        return pl.pallas_call(
+            lambda in_ref, out_ref: out_ref.__setitem__(0, in_ref[...]),
+            grid=(1,),
+            in_specs=[pl.BlockSpec((pairs, piece, COLUMNS), lambda i: (0, r, j))],
+            out_specs=pl.BlockSpec((1, pairs, piece, COLUMNS), lambda i: (0, 0, 0, 0)),
+            out_shape=jax.ShapeDtypeStruct((1, pairs, piece, COLUMNS), amplitude.dtype),
+            name="first_piece",
+        )(amplitude)
 
     def kernel(in_ref, out_ref):
         for n, (j, r) in enumerate(members):
@@ -257,7 +266,9 @@
                 other = lax.ppermute(own, "core", [(i, 1 - i) for i in range(nc)])
                 around, index = [own, other], own_index
             else:
-                around, index = [lax.all_gather(block, ("z", "core"), axis=0)], all_index
+                everyone = lax.all_gather(block, ("z", "core"), axis=0)
+                everyone, _ = lax.optimization_barrier((everyone, leaving))
+                around, index = [everyone], all_index
         for n, member in enumerate(members):
             with jax.named_scope("along_y"):
                 stay, ahead, far, back = pick(around, n, index, ny, "pick_y")

time: 263 us -> 269 us (1.023)
  waiting for transfers between devices: 90.5 us -> 102 us
  starting transfers between devices: 79.7 us -> 75.2 us
    ppermute x18, waiting for transfers between devices: 5.92 us -> 27.6 us  [shift(): return lax.ppermute(array, 'y', [(i, (i + step) % ny) for i in range(ny)])]
    all_gather x1, waiting for transfers between devices: 12.2 us -> 0.02 us  [per_device(): everyone = lax.all_gather(block, ('z', 'core'), axis=0)]
    all_to_all x6, waiting for transfers between devices: 33.6 us -> 41.2 us  [per_device(): arrived = lax.all_to_all(leaving, 'dom', 0, 0, tiled=True)]
    ppermute x8, waiting for transfers between devices: 16.1 us -> 9.2 us  [shift(): lax.ppermute(array, 'z', [(i, (i + step) % count) for i in range(count)])]
    ppermute x18, starting transfers between devices: 25 us -> 20.1 us  [shift(): return lax.ppermute(array, 'y', [(i, (i + step) % ny) for i in range(ny)])]
  transfers between devices with their start and end apart: 35 -> 35, of which waited for: 17 -> 14; matrix products, arithmetic and copies ran while one was open for 1% -> 1% of each run, Pallas kernels for 20% -> 18%
where the time goes in v3:
time: 269 us; the launch traced here: 268 us
  waiting for transfers between devices  102 us (38%)
  starting transfers between devices  75.2 us (28%)
  Pallas kernels  66.7 us (25%)
  between operations  14.5 us (5%)
  local copies, waits for them, and re-layouts  5.69 us (2%)
  other arithmetic  3.59 us (1%)
    all_to_all x6, waiting for transfers between devices, per_device(): arrived = lax.all_to_all(leaving, 'dom', 0, 0, tiled=True)  41.2 us
    pallas_call x12, Pallas kernels, pick(): pl.pallas_call(kernel, in_specs=[pl.BlockSpec(memory_space=pltpu.SMEM)] +...  38.6 us
    all_to_all x6, starting transfers between devices, per_device(): arrived = lax.all_to_all(leaving, 'dom', 0, 0, tiled=True)  32.7 us
    ppermute x18, waiting for transfers between devices, shift(): return lax.ppermute(array, 'y', [(i, (i + step) % ny) for i in range(ny)])  27.6 us
    pallas_call x2, Pallas kernels, per_device(): total = couple(*args)  24.6 us
    all_to_all x1, waiting for transfers between devices, per_device(): shares = lax.all_to_all(total, 'dom', 0, 0, tiled=True)  22.7 us
    ppermute x18, starting transfers between devices, shift(): return lax.ppermute(array, 'y', [(i, (i + step) % ny) for i in range(ny)])  20.1 us
    ppermute x8, starting transfers between devices, shift(): lax.ppermute(array, 'z', [(i, (i + step) % count) for i in range(count)])  17.2 us
  transfers between devices with their start and end apart: 35, of which 14 were waited for; matrix products, arithmetic and copies ran while one was open for 1% of the time, Pallas kernels for 18%

profile of v3, /device:TPU:2, one launch (start us, length us, event | category | flops | bytes accessed | tf_op | source)
XLA Modules:
  0.0 267.9 jit_solution(15458219182807970777)
XLA Ops:
  7.2 2.0 split.1
  9.2 1.5 first_piece.1
  10.8 1.9 collective-permute-start
  12.7 3.9 %collective-permute-start.1 = (bf16[1,8,48,128]{3,2,1,0:T(8,128)(2,1)}, bf16[1,8,48,128]{3,2,1,0:T(8,128)(2,1)S(1)}, u32[]{:S(2)}, u32[]{:S(2)}) collective-permute-start(bf16[1,8,48,128]{3,2,1,0:T(8,128)(2,1)} %first_piece.1), channel_id=1, source_target_pairs={{0,56},{8,0},{16,8},{24,16},{32,24},{40,32},{48,40},{56,48},{1,57}... | collective-permute-start | bytes 294920 | tf_op jit(solution)/shard_map/along_z/ppermute | solution.py:30
  16.6 4.1 %collective-permute-start.3 = (bf16[1,8,48,128]{3,2,1,0:T(8,128)(2,1)}, bf16[1,8,48,128]{3,2,1,0:T(8,128)(2,1)S(1)}, u32[]{:S(2)}, u32[]{:S(2)}) collective-permute-start(bf16[1,8,48,128]{3,2,1,0:T(8,128)(2,1)} %first_piece.1), channel_id=1, source_target_pairs={{0,48},{8,56},{16,0},{24,8},{32,16},{40,24},{48,32},{56,40},{1,49}... | collective-permute-start | bytes 294920 | tf_op jit(solution)/shard_map/along_z/ppermute | solution.py:30
  21.6 0.9 bitcast_dynamic-update-slice_fusion.6
  22.5 3.2 %collective-permute-done.3 = bf16[1,8,48,128]{3,2,1,0:T(8,128)(2,1)S(1)} collective-permute-done((bf16[1,8,48,128]{3,2,1,0:T(8,128)(2,1)}, bf16[1,8,48,128]{3,2,1,0:T(8,128)(2,1)S(1)}, u32[]{:S(2)}, u32[]{:S(2)}) %collective-permute-start.3) | collective-permute-done | bytes 98336 | tf_op jit(solution)/shard_map/along_z/ppermute | solution.py:30
  25.7 2.4 collective-permute-start.7
  28.1 1.6 collective-permute-start.6
  29.7 3.2 %collective-permute-start.5 = (bf16[1,8,48,128]{3,2,1,0:T(8,128)(2,1)S(1)}, bf16[1,8,48,128]{3,2,1,0:T(8,128)(2,1)S(1)}, u32[]{:S(2)}, u32[]{:S(2)}) collective-permute-start(bf16[1,8,48,128]{3,2,1,0:T(8,128)(2,1)S(1)} %collective-permute-done.3), channel_id=1, source_target_pairs={{0,56},{8,0},{16,8},{24,16},{32,24},{40,32},{48,40},{56,48},{1,57}... | collective-permute-start | bytes 294920 | tf_op jit(solution)/shard_map/along_z/ppermute | solution.py:30
  33.0 5.5 %collective-permute-done.4 = bf16[1,8,48,128]{3,2,1,0:T(8,128)(2,1)S(1)} collective-permute-done((bf16[1,8,48,128]{3,2,1,0:T(8,128)(2,1)S(1)}, bf16[1,8,48,128]{3,2,1,0:T(8,128)(2,1)S(1)}, u32[]{:S(2)}, u32[]{:S(2)}) %collective-permute-start.4) | collective-permute-done | bytes 98336 | tf_op jit(solution)/shard_map/along_z/ppermute | solution.py:30
  38.5 0.5 collective-permute-done.5
  40.1 1.4 collective-permute-done.8.refs_1_
  41.5 0.9 copy-done.9
  42.4 2.3 pick_y.6
  44.7 3.2 %collective-permute-start.9 = (bf16[32,48,128]{2,1,0:T(8,128)(2,1)S(1)}, bf16[32,48,128]{2,1,0:T(8,128)(2,1)S(1)}, u32[]{:S(2)}, u32[]{:S(2)}) collective-permute-start(bf16[32,48,128]{2,1,0:T(8,128)(2,1)S(1)} %get-tuple-element.28), channel_id=1, source_target_pairs={{0,192},{64,0},{128,64},{192,128},{1,193},{65,1},{129,65},{193,129... | collective-permute-start | bytes 1179656 | tf_op jit(solution)/shard_map/along_y/ppermute | solution.py:257
  47.9 0.6 collective-permute-start.10
  48.5 1.0 collective-permute-start.11
  49.7 15.3 %collective-permute-done.9 = bf16[32,48,128]{2,1,0:T(8,128)(2,1)S(1)} collective-permute-done((bf16[32,48,128]{2,1,0:T(8,128)(2,1)S(1)}, bf16[32,48,128]{2,1,0:T(8,128)(2,1)S(1)}, u32[]{:S(2)}, u32[]{:S(2)}) %collective-permute-start.9) | collective-permute-done | bytes 393248 | tf_op jit(solution)/shard_map/along_y/ppermute | solution.py:257
  65.0 3.7 %collective-permute-done.11 = bf16[32,48,128]{2,1,0:T(8,128)(2,1)S(1)} collective-permute-done((bf16[32,48,128]{2,1,0:T(8,128)(2,1)S(1)}, bf16[32,48,128]{2,1,0:T(8,128)(2,1)S(1)}, u32[]{:S(2)}, u32[]{:S(2)}) %collective-permute-start.11) | collective-permute-done | bytes 393248 | tf_op jit(solution)/shard_map/along_y/ppermute | solution.py:257
  68.6 2.7 %pick_x.6 = bf16[128,48,128]{2,1,0:T(8,128)(2,1)} custom-call(s32[128]{0:T(128)S(1)} %fusion.11.index_ref, bf16[1,1,32,48,128]{4,3,2,1,0:T(8,128)(2,1)S(1)} %bitcast.67, bf16[1,1,32,48,128]{4,3,2,1,0:T(8,128)(2,1)S(1)} %bitcast.68, bf16[1,1,32,48,128]{4,3,2,1,0:T(8,128)(2,1)S(1)} %bitcast.69, bf16[1,1,32,48,128]{4,3,2,1,0:T(8,128)(2,1)S(1)} %bitcast.70), custom_call_target="tpu_custom_call" | custom-call | flops 12000000000 | bytes 36000000 | tf_op jit(solution)/shard_map/along_x/pick_x/pallas_call | solution.py:99
  71.4 3.2 %pick_y.7 = (bf16[32,48,128]{2,1,0:T(8,128)(2,1)S(1)}, bf16[32,48,128]{2,1,0:T(8,128)(2,1)S(1)}, bf16[32,48,128]{2,1,0:T(8,128)(2,1)}, bf16[32,48,128]{2,1,0:T(8,128)(2,1)}) custom-call(s32[128]{0:T(128)S(1)} %get-tuple-element.59.index_ref, bf16[16,5,8,48,128]{4,3,2,1,0:T(8,128)(2,1)} %bitcast.71), custom_call_target="tpu_custom_call" | custom-call | tf_op jit(solution)/shard_map/along_y/pick_y/pallas_call | solution.py:99
  74.5 2.0 collective-permute-start.12
  76.5 0.8 collective-permute-start.13
  77.3 0.9 collective-permute-start.14
  78.2 4.8 %all-to-all-start.2 = ((bf16[128,48,128]{2,1,0:T(8,128)(2,1)}), bf16[128,48,128]{2,1,0:T(8,128)(2,1)S(1)}, u32[]{:S(2)}, u32[]{:S(2)}) async-start(bf16[128,48,128]{2,1,0:T(8,128)(2,1)} %pick_x.6), calls=%async_computation.2 | async-start | bytes 3145728 | tf_op jit(solution)/shard_map/along_x/all_to_all | solution.py:281
  83.0 3.3 %pick_y.9 = (bf16[32,48,128]{2,1,0:T(8,128)(2,1)S(1)}, bf16[32,48,128]{2,1,0:T(8,128)(2,1)}, bf16[32,48,128]{2,1,0:T(8,128)(2,1)}, bf16[32,48,128]{2,1,0:T(8,128)(2,1)}) custom-call(s32[128]{0:T(128)S(1)} %get-tuple-element.59.index_ref, bf16[16,5,8,48,128]{4,3,2,1,0:T(8,128)(2,1)} %bitcast.72), custom_call_target="tpu_custom_call" | custom-call | tf_op jit(solution)/shard_map/along_y/pick_y/pallas_call | solution.py:99
  86.3 2.4 collective-permute-start.18
  88.7 1.5 collective-permute-start.19
  90.2 3.8 %collective-permute-done.12 = bf16[32,48,128]{2,1,0:T(8,128)(2,1)S(1)} collective-permute-done((bf16[32,48,128]{2,1,0:T(8,128)(2,1)}, bf16[32,48,128]{2,1,0:T(8,128)(2,1)S(1)}, u32[]{:S(2)}, u32[]{:S(2)}) %collective-permute-start.12) | collective-permute-done | bytes 393248 | tf_op jit(solution)/shard_map/along_y/ppermute | solution.py:257
  94.0 4.8 %collective-permute-done.14 = bf16[32,48,128]{2,1,0:T(8,128)(2,1)} collective-permute-done((bf16[32,48,128]{2,1,0:T(8,128)(2,1)S(1)}, bf16[32,48,128]{2,1,0:T(8,128)(2,1)}, u32[]{:S(2)}, u32[]{:S(2)}) %collective-permute-start.14) | collective-permute-done | bytes 393248 | tf_op jit(solution)/shard_map/along_y/ppermute | solution.py:257
  98.8 3.5 %pick_x.7 = bf16[128,48,128]{2,1,0:T(8,128)(2,1)} custom-call(s32[128]{0:T(128)S(1)} %fusion.11.index_ref, bf16[1,1,32,48,128]{4,3,2,1,0:T(8,128)(2,1)S(1)} %bitcast.64, bf16[1,1,32,48,128]{4,3,2,1,0:T(8,128)(2,1)S(1)} %bitcast.65, bf16[1,1,32,48,128]{4,3,2,1,0:T(8,128)(2,1)S(1)} %bitcast.66, bf16[1,1,32,48,128]{4,3,2,1,0:T(8,128)(2,1)} %bitcast.22.refs_3_), custom_call_target="tpu_custom_call" | custom-call | flops 12000000000 | bytes 36000000 | tf_op jit(solution)/shard_map/along_x/pick_x/pallas_call | solution.py:99
  102.4 4.8 %all-to-all-start = ((bf16[128,48,128]{2,1,0:T(8,128)(2,1)}), bf16[128,48,128]{2,1,0:T(8,128)(2,1)S(1)}, u32[]{:S(2)}, u32[]{:S(2)}) async-start(bf16[128,48,128]{2,1,0:T(8,128)(2,1)} %pick_x.7), calls=%async_computation | async-start | bytes 3145728 | tf_op jit(solution)/shard_map/along_x/all_to_all | solution.py:281
  107.2 3.3 %pick_y.10 = (bf16[32,48,128]{2,1,0:T(8,128)(2,1)S(1)}, bf16[32,48,128]{2,1,0:T(8,128)(2,1)}, bf16[32,48,128]{2,1,0:T(8,128)(2,1)}, bf16[32,48,128]{2,1,0:T(8,128)(2,1)}) custom-call(s32[128]{0:T(128)S(1)} %get-tuple-element.59.index_ref, bf16[16,5,8,48,128]{4,3,2,1,0:T(8,128)(2,1)} %bitcast.73), custom_call_target="tpu_custom_call" | custom-call | tf_op jit(solution)/shard_map/along_y/pick_y/pallas_call | solution.py:99
  110.5 0.7 copy-done.5
  111.3 2.0 collective-permute-start.21
  113.2 1.5 collective-permute-start.22
  114.7 3.3 %pick_x.9 = bf16[128,48,128]{2,1,0:T(8,128)(2,1)} custom-call(s32[128]{0:T(128)S(1)} %fusion.11.index_ref, bf16[1,1,32,48,128]{4,3,2,1,0:T(8,128)(2,1)S(1)} %bitcast.62, bf16[1,1,32,48,128]{4,3,2,1,0:T(8,128)(2,1)} %bitcast.31.refs_1_, bf16[1,1,32,48,128]{4,3,2,1,0:T(8,128)(2,1)} %bitcast.32.refs_2_, bf16[1,1,32,48,128]{4,3,2,1,0:T(8,128)(2,1)} %bitcast.33.refs_3_), custom_call_target="tpu_custom_call" | custom-call | flops 12000000000 | bytes 36000000 | tf_op jit(solution)/shard_map/along_x/pick_x/pallas_call | solution.py:99
  118.1 8.3 %all-to-all-done = bf16[128,48,128]{2,1,0:T(8,128)(2,1)S(1)} async-done(((bf16[128,48,128]{2,1,0:T(8,128)(2,1)}), bf16[128,48,128]{2,1,0:T(8,128)(2,1)S(1)}, u32[]{:S(2)}, u32[]{:S(2)}) %all-to-all-start) | async-done | bytes 1572896 | tf_op jit(solution)/shard_map/along_x/all_to_all | solution.py:281
  126.4 5.8 %all-to-all-start.3 = ((bf16[128,48,128]{2,1,0:T(8,128)(2,1)}), bf16[128,48,128]{2,1,0:T(8,128)(2,1)}, u32[]{:S(2)}, u32[]{:S(2)}) async-start(bf16[128,48,128]{2,1,0:T(8,128)(2,1)} %pick_x.9), calls=%async_computation.3 | async-start | bytes 3145728 | tf_op jit(solution)/shard_map/along_x/all_to_all | solution.py:281
  132.2 3.3 %pick_y.11 = (bf16[32,48,128]{2,1,0:T(8,128)(2,1)S(1)}, bf16[32,48,128]{2,1,0:T(8,128)(2,1)}, bf16[32,48,128]{2,1,0:T(8,128)(2,1)}, bf16[32,48,128]{2,1,0:T(8,128)(2,1)}) custom-call(s32[128]{0:T(128)S(1)} %get-tuple-element.59.index_ref, bf16[16,5,8,48,128]{4,3,2,1,0:T(8,128)(2,1)} %bitcast.74), custom_call_target="tpu_custom_call" | custom-call | tf_op jit(solution)/shard_map/along_y/pick_y/pallas_call | solution.py:99
  135.5 0.7 copy-done.3
  136.3 0.7 collective-permute-start.24
  136.9 1.5 collective-permute-start.25
  138.5 3.4 %pick_x.10 = bf16[128,48,128]{2,1,0:T(8,128)(2,1)} custom-call(s32[128]{0:T(128)S(1)} %fusion.11.index_ref, bf16[1,1,32,48,128]{4,3,2,1,0:T(8,128)(2,1)S(1)} %bitcast.63, bf16[1,1,32,48,128]{4,3,2,1,0:T(8,128)(2,1)} %bitcast.36.refs_1_, bf16[1,1,32,48,128]{4,3,2,1,0:T(8,128)(2,1)} %bitcast.37.refs_2_, bf16[1,1,32,48,128]{4,3,2,1,0:T(8,128)(2,1)} %bitcast.38.refs_3_), custom_call_target="tpu_custom_call" | custom-call | flops 12000000000 | bytes 36000000 | tf_op jit(solution)/shard_map/along_x/pick_x/pallas_call | solution.py:99
  142.0 8.7 %all-to-all-done.3 = bf16[128,48,128]{2,1,0:T(8,128)(2,1)} async-done(((bf16[128,48,128]{2,1,0:T(8,128)(2,1)}), bf16[128,48,128]{2,1,0:T(8,128)(2,1)}, u32[]{:S(2)}, u32[]{:S(2)}) %all-to-all-start.3) | async-done | bytes 1572896 | tf_op jit(solution)/shard_map/along_x/all_to_all | solution.py:281
  150.6 5.8 %all-to-all-start.4 = ((bf16[128,48,128]{2,1,0:T(8,128)(2,1)}), bf16[128,48,128]{2,1,0:T(8,128)(2,1)}, u32[]{:S(2)}, u32[]{:S(2)}) async-start(bf16[128,48,128]{2,1,0:T(8,128)(2,1)} %pick_x.10), calls=%async_computation.4 | async-start | bytes 3145728 | tf_op jit(solution)/shard_map/along_x/all_to_all | solution.py:281
  156.4 3.3 %pick_y.8 = (bf16[32,48,128]{2,1,0:T(8,128)(2,1)S(1)}, bf16[32,48,128]{2,1,0:T(8,128)(2,1)}, bf16[32,48,128]{2,1,0:T(8,128)(2,1)}, bf16[32,48,128]{2,1,0:T(8,128)(2,1)}) custom-call(s32[128]{0:T(128)S(1)} %get-tuple-element.59.index_ref, bf16[16,5,8,48,128]{4,3,2,1,0:T(8,128)(2,1)} %bitcast.75), custom_call_target="tpu_custom_call" | custom-call | tf_op jit(solution)/shard_map/along_y/pick_y/pallas_call | solution.py:99
  159.8 0.8 collective-permute-start.16
  160.6 1.2 collective-permute-start.17
  161.8 3.4 %pick_x.11 = bf16[128,48,128]{2,1,0:T(8,128)(2,1)} custom-call(s32[128]{0:T(128)S(1)} %fusion.11.index_ref, bf16[1,1,32,48,128]{4,3,2,1,0:T(8,128)(2,1)S(1)} %bitcast.61, bf16[1,1,32,48,128]{4,3,2,1,0:T(8,128)(2,1)} %bitcast.41.refs_1_, bf16[1,1,32,48,128]{4,3,2,1,0:T(8,128)(2,1)} %bitcast.42.refs_2_, bf16[1,1,32,48,128]{4,3,2,1,0:T(8,128)(2,1)} %bitcast.43.refs_3_), custom_call_target="tpu_custom_call" | custom-call | flops 12000000000 | bytes 36000000 | tf_op jit(solution)/shard_map/along_x/pick_x/pallas_call | solution.py:99
  165.2 8.7 %all-to-all-done.4 = bf16[128,48,128]{2,1,0:T(8,128)(2,1)} async-done(((bf16[128,48,128]{2,1,0:T(8,128)(2,1)}), bf16[128,48,128]{2,1,0:T(8,128)(2,1)}, u32[]{:S(2)}, u32[]{:S(2)}) %all-to-all-start.4) | async-done | bytes 1572896 | tf_op jit(solution)/shard_map/along_x/all_to_all | solution.py:281
  174.0 5.8 %all-to-all-start.5 = ((bf16[128,48,128]{2,1,0:T(8,128)(2,1)}), bf16[128,48,128]{2,1,0:T(8,128)(2,1)}, u32[]{:S(2)}, u32[]{:S(2)}) async-start(bf16[128,48,128]{2,1,0:T(8,128)(2,1)} %pick_x.11), calls=%async_computation.5 | async-start | bytes 3145728 | tf_op jit(solution)/shard_map/along_x/all_to_all | solution.py:281
  179.8 0.8 dynamic_slice.24
  180.5 3.4 %pick_x.8 = bf16[128,48,128]{2,1,0:T(8,128)(2,1)} custom-call(s32[128]{0:T(128)S(1)} %fusion.11.index_ref, bf16[1,1,32,48,128]{4,3,2,1,0:T(8,128)(2,1)S(1)} %bitcast.60, bf16[1,1,32,48,128]{4,3,2,1,0:T(8,128)(2,1)} %bitcast.25.refs_1_, bf16[1,1,32,48,128]{4,3,2,1,0:T(8,128)(2,1)} %bitcast.26.refs_2_, bf16[1,1,32,48,128]{4,3,2,1,0:T(8,128)(2,1)} %bitcast.27.refs_3_), custom_call_target="tpu_custom_call" | custom-call | flops 12000000000 | bytes 36000000 | tf_op jit(solution)/shard_map/along_x/pick_x/pallas_call | solution.py:99
  184.0 12.4 %all-to-all-done.5 = bf16[128,48,128]{2,1,0:T(8,128)(2,1)} async-done(((bf16[128,48,128]{2,1,0:T(8,128)(2,1)}), bf16[128,48,128]{2,1,0:T(8,128)(2,1)}, u32[]{:S(2)}, u32[]{:S(2)}) %all-to-all-start.5) | async-done | bytes 1572896 | tf_op jit(solution)/shard_map/along_x/all_to_all | solution.py:281
  196.4 5.8 %all-to-all-start.1 = ((bf16[128,48,128]{2,1,0:T(8,128)(2,1)}), bf16[128,48,128]{2,1,0:T(8,128)(2,1)}, u32[]{:S(2)}, u32[]{:S(2)}) async-start(bf16[128,48,128]{2,1,0:T(8,128)(2,1)} %pick_x.8), calls=%async_computation.1 | async-start | bytes 3145728 | tf_op jit(solution)/shard_map/along_x/all_to_all | solution.py:281
  202.4 12.4 %couple.2.rest_2_ = f32[8,384,384]{2,1,0:T(8,128)} custom-call(s32[32]{0:T(128)S(1)} %and_select_fusion.4.target, f32[32]{0:T(128)S(1)} %copy-done.2, bf16[32,384,384]{2,1,0:T(8,128)(2,1)} %s_ref.3, bf16[4,32,48,128]{3,2,1,0:T(8,128)(2,1)S(1)} %bitcast.59, bf16[4,32,48,128]{3,2,1,0:T(8,128)(2,1)} %bitcast.34.rest_1_, ...), custom_call_target="tpu_custom_call" | custom-call | flops 9663676416 | bytes 14155776 | tf_op jit(solution)/shard_map/couple/couple/pallas_call | solution.py:292
  214.8 3.1 %all-to-all-done.1 = bf16[128,48,128]{2,1,0:T(8,128)(2,1)} async-done(((bf16[128,48,128]{2,1,0:T(8,128)(2,1)}), bf16[128,48,128]{2,1,0:T(8,128)(2,1)}, u32[]{:S(2)}, u32[]{:S(2)}) %all-to-all-start.1) | async-done | bytes 1572896 | tf_op jit(solution)/shard_map/along_x/all_to_all | solution.py:281
  217.9 12.2 %couple.3 = bf16[4,8,96,384]{3,2,1,0:T(8,128)(2,1)} custom-call(s32[32]{0:T(128)S(1)} %and_select_fusion.4.target, f32[32]{0:T(128)S(1)} %copy-done.2, bf16[32,384,384]{2,1,0:T(8,128)(2,1)} %s_ref.3, bf16[4,32,48,128]{3,2,1,0:T(8,128)(2,1)S(1)} %bitcast.58, bf16[4,32,48,128]{3,2,1,0:T(8,128)(2,1)} %bitcast.28.rest_1_, f32[8,384,384]{2,1,0:T(8,128)} %couple.2.rest_2_), custom_call_target="tpu_custom_call" | custom-call | flops 4831838208 | bytes 14155776 | tf_op jit(solution)/shard_map/couple/couple/pallas_call | solution.py:292
  230.2 5.1 %all-to-all-start.6 = ((bf16[4,8,96,384]{3,2,1,0:T(8,128)(2,1)}), bf16[4,8,96,384]{3,2,1,0:T(8,128)(2,1)S(1)}, u32[]{:S(2)}, u32[]{:S(2)}) async-start(bf16[4,8,96,384]{3,2,1,0:T(8,128)(2,1)} %couple.3), calls=%async_computation.6 | async-start | bytes 4718592 | tf_op jit(solution)/shard_map/sum_x/all_to_all | solution.py:294
  235.3 22.7 %all-to-all-done.6 = bf16[4,8,96,384]{3,2,1,0:T(8,128)(2,1)S(1)} async-done(((bf16[4,8,96,384]{3,2,1,0:T(8,128)(2,1)}), bf16[4,8,96,384]{3,2,1,0:T(8,128)(2,1)S(1)}, u32[]{:S(2)}, u32[]{:S(2)}) %all-to-all-start.6) | async-done | bytes 2359328 | tf_op jit(solution)/shard_map/sum_x/all_to_all | solution.py:294
  258.4 0.7 copy-done.10
  259.1 1.9 convert_subtract_fusion
  (92 shorter events, 3.0 us)
Async XLA Ops:
  7.2 13.6 %copy-start = (s32[8192]{0:T(1024)S(1)}, s32[8192]{0:T(1024)}, u32[]{:S(2)}) copy-start(s32[8192]{0:T(1024)} %param.15) | copy-start | bytes 98308
  7.2 13.6 %copy-start.14 = (s32[8]{0:T(128)S(1)}, s32[8]{0:T(128)}, u32[]{:S(2)}) copy-start(s32[8]{0:T(128)} %constant.177.clone) | copy-start | bytes 100
  7.2 13.8 %copy-start.12 = (s32[512]{0:T(512)S(1)}, s32[512]{0:T(512)}, u32[]{:S(2)}) copy-start(s32[512]{0:T(512)} %param.14) | copy-start | bytes 6148
  7.2 64.2 %all-gather.3.cloned.1.call-start = ((), (), s32[]{:S(2)}) async-start(), calls=%async_computation.7 | async-start | bytes 8355840 | tf_op jit(solution)/shard_map/along_z/all_gather | solution.py:269
  10.8 18.9 %collective-permute-start = (bf16[1,8,48,128]{3,2,1,0:T(8,128)(2,1)}, bf16[1,8,48,128]{3,2,1,0:T(8,128)(2,1)S(1)}, u32[]{:S(2)}, u32[]{:S(2)}) collective-permute-start(bf16[1,8,48,128]{3,2,1,0:T(8,128)(2,1)} %first_piece.1), channel_id=1, source_target_pairs={{0,8},{8,16},{16,24},{24,32},{32,40},{40,48},{48,56},{56,0},{1,9},... | collective-permute-start | bytes 294920 | tf_op jit(solution)/shard_map/along_z/ppermute | solution.py:30
  12.7 20.3 %collective-permute-start.1 = (bf16[1,8,48,128]{3,2,1,0:T(8,128)(2,1)}, bf16[1,8,48,128]{3,2,1,0:T(8,128)(2,1)S(1)}, u32[]{:S(2)}, u32[]{:S(2)}) collective-permute-start(bf16[1,8,48,128]{3,2,1,0:T(8,128)(2,1)} %first_piece.1), channel_id=1, source_target_pairs={{0,56},{8,0},{16,8},{24,16},{32,24},{40,32},{48,40},{56,48},{1,57}... | collective-permute-start | bytes 294920 | tf_op jit(solution)/shard_map/along_z/ppermute | solution.py:30
  16.6 11.5 %collective-permute-start.2 = (bf16[1,8,48,128]{3,2,1,0:T(8,128)(2,1)}, bf16[1,8,48,128]{3,2,1,0:T(8,128)(2,1)S(1)}, u32[]{:S(2)}, u32[]{:S(2)}) collective-permute-start(bf16[1,8,48,128]{3,2,1,0:T(8,128)(2,1)} %first_piece.1), channel_id=1, source_target_pairs={{0,16},{8,24},{16,32},{24,40},{32,48},{40,56},{48,0},{56,8},{1,17}... | collective-permute-start | bytes 294920 | tf_op jit(solution)/shard_map/along_z/ppermute | solution.py:30
  16.6 9.1 %collective-permute-start.3 = (bf16[1,8,48,128]{3,2,1,0:T(8,128)(2,1)}, bf16[1,8,48,128]{3,2,1,0:T(8,128)(2,1)S(1)}, u32[]{:S(2)}, u32[]{:S(2)}) collective-permute-start(bf16[1,8,48,128]{3,2,1,0:T(8,128)(2,1)} %first_piece.1), channel_id=1, source_target_pairs={{0,48},{8,56},{16,0},{24,8},{32,16},{40,24},{48,32},{56,40},{1,49}... | collective-permute-start | bytes 294920 | tf_op jit(solution)/shard_map/along_z/ppermute | solution.py:30
  25.7 13.3 %collective-permute-start.7 = (bf16[1,4,48,128]{3,2,1,0:T(8,128)(2,1)S(1)}, bf16[1,4,48,128]{3,2,1,0:T(8,128)(2,1)S(1)}, u32[]{:S(2)}, u32[]{:S(2)}) collective-permute-start(bf16[1,4,48,128]{3,2,1,0:T(8,128)(2,1)S(1)} %slice.9), channel_id=1, source_target_pairs={{0,48},{8,56},{16,0},{24,8},{32,16},{40,24},{48,32},{56,40},{1,49}... | collective-permute-start | bytes 147464 | tf_op jit(solution)/shard_map/along_z/ppermute | solution.py:30
  28.1 10.9 %collective-permute-start.6 = (bf16[1,4,48,128]{3,2,1,0:T(8,128)(2,1)S(1)}, bf16[1,4,48,128]{3,2,1,0:T(8,128)(2,1)S(1)}, u32[]{:S(2)}, u32[]{:S(2)}) collective-permute-start(bf16[1,4,48,128]{3,2,1,0:T(8,128)(2,1)S(1)} %slice.8), channel_id=1, source_target_pairs={{0,16},{8,24},{16,32},{24,40},{32,48},{40,56},{48,0},{56,8},{1,17}... | collective-permute-start | bytes 147464 | tf_op jit(solution)/shard_map/along_z/ppermute | solution.py:30
  29.7 8.8 %collective-permute-start.4 = (bf16[1,8,48,128]{3,2,1,0:T(8,128)(2,1)S(1)}, bf16[1,8,48,128]{3,2,1,0:T(8,128)(2,1)S(1)}, u32[]{:S(2)}, u32[]{:S(2)}) collective-permute-start(bf16[1,8,48,128]{3,2,1,0:T(8,128)(2,1)S(1)} %collective-permute-done.2), channel_id=1, source_target_pairs={{0,8},{8,16},{16,24},{24,32},{32,40},{40,48},{48,56},{56,0},{1,9},... | collective-permute-start | bytes 294920 | tf_op jit(solution)/shard_map/along_z/ppermute | solution.py:30
  29.7 9.3 %collective-permute-start.5 = (bf16[1,8,48,128]{3,2,1,0:T(8,128)(2,1)S(1)}, bf16[1,8,48,128]{3,2,1,0:T(8,128)(2,1)S(1)}, u32[]{:S(2)}, u32[]{:S(2)}) collective-permute-start(bf16[1,8,48,128]{3,2,1,0:T(8,128)(2,1)S(1)} %collective-permute-done.3), channel_id=1, source_target_pairs={{0,56},{8,0},{16,8},{24,16},{32,24},{40,32},{48,40},{56,48},{1,57}... | collective-permute-start | bytes 294920 | tf_op jit(solution)/shard_map/along_z/ppermute | solution.py:30
  39.1 2.4 copy-start.8
  39.1 2.4 collective-permute-start.8
  41.5 0.9 copy-start.9
  44.7 20.2 %collective-permute-start.9 = (bf16[32,48,128]{2,1,0:T(8,128)(2,1)S(1)}, bf16[32,48,128]{2,1,0:T(8,128)(2,1)S(1)}, u32[]{:S(2)}, u32[]{:S(2)}) collective-permute-start(bf16[32,48,128]{2,1,0:T(8,128)(2,1)S(1)} %get-tuple-element.28), channel_id=1, source_target_pairs={{0,192},{64,0},{128,64},{192,128},{1,193},{65,1},{129,65},{193,129... | collective-permute-start | bytes 1179656 | tf_op jit(solution)/shard_map/along_y/ppermute | solution.py:257
  47.9 17.1 %collective-permute-start.10 = (bf16[32,48,128]{2,1,0:T(8,128)(2,1)S(1)}, bf16[32,48,128]{2,1,0:T(8,128)(2,1)S(1)}, u32[]{:S(2)}, u32[]{:S(2)}) collective-permute-start(bf16[32,48,128]{2,1,0:T(8,128)(2,1)S(1)} %get-tuple-element.29), channel_id=1, source_target_pairs={{0,128},{64,192},{128,0},{192,64},{1,129},{65,193},{129,1},{193,65... | collective-permute-start | bytes 1179656 | tf_op jit(solution)/shard_map/along_y/ppermute | solution.py:257
  48.5 20.2 %collective-permute-start.11 = (bf16[32,48,128]{2,1,0:T(8,128)(2,1)S(1)}, bf16[32,48,128]{2,1,0:T(8,128)(2,1)S(1)}, u32[]{:S(2)}, u32[]{:S(2)}) collective-permute-start(bf16[32,48,128]{2,1,0:T(8,128)(2,1)S(1)} %get-tuple-element.30), channel_id=1, source_target_pairs={{0,64},{64,128},{128,192},{192,0},{1,65},{65,129},{129,193},{193,1... | collective-permute-start | bytes 1179656 | tf_op jit(solution)/shard_map/along_y/ppermute | solution.py:257
  74.5 19.5 %collective-permute-start.12 = (bf16[32,48,128]{2,1,0:T(8,128)(2,1)}, bf16[32,48,128]{2,1,0:T(8,128)(2,1)S(1)}, u32[]{:S(2)}, u32[]{:S(2)}) collective-permute-start(bf16[32,48,128]{2,1,0:T(8,128)(2,1)} %get-tuple-element.33), channel_id=1, source_target_pairs={{0,192},{64,0},{128,64},{192,128},{1,193},{65,1},{129,65},{193,129... | collective-permute-start | bytes 1179656 | tf_op jit(solution)/shard_map/along_y/ppermute | solution.py:257
  76.5 17.5 %collective-permute-start.13 = (bf16[32,48,128]{2,1,0:T(8,128)(2,1)}, bf16[32,48,128]{2,1,0:T(8,128)(2,1)S(1)}, u32[]{:S(2)}, u32[]{:S(2)}) collective-permute-start(bf16[32,48,128]{2,1,0:T(8,128)(2,1)} %get-tuple-element.34), channel_id=1, source_target_pairs={{0,128},{64,192},{128,0},{192,64},{1,129},{65,193},{129,1},{193,65... | collective-permute-start | bytes 1179656 | tf_op jit(solution)/shard_map/along_y/ppermute | solution.py:257
  77.3 21.5 %collective-permute-start.14 = (bf16[32,48,128]{2,1,0:T(8,128)(2,1)S(1)}, bf16[32,48,128]{2,1,0:T(8,128)(2,1)}, u32[]{:S(2)}, u32[]{:S(2)}) collective-permute-start(bf16[32,48,128]{2,1,0:T(8,128)(2,1)S(1)} %get-tuple-element.35), channel_id=1, source_target_pairs={{0,64},{64,128},{128,192},{192,0},{1,65},{65,129},{129,193},{193,1... | collective-permute-start | bytes 1179656 | tf_op jit(solution)/shard_map/along_y/ppermute | solution.py:257
  78.2 24.2 %all-to-all-start.2 = ((bf16[128,48,128]{2,1,0:T(8,128)(2,1)}), bf16[128,48,128]{2,1,0:T(8,128)(2,1)S(1)}, u32[]{:S(2)}, u32[]{:S(2)}) async-start(bf16[128,48,128]{2,1,0:T(8,128)(2,1)} %pick_x.6), calls=%async_computation.2 | async-start | bytes 3145728 | tf_op jit(solution)/shard_map/along_x/all_to_all | solution.py:281
  86.3 28.5 %collective-permute-start.18 = (bf16[32,48,128]{2,1,0:T(8,128)(2,1)}, bf16[32,48,128]{2,1,0:T(8,128)(2,1)}, u32[]{:S(2)}, u32[]{:S(2)}) collective-permute-start(bf16[32,48,128]{2,1,0:T(8,128)(2,1)} %get-tuple-element.41), channel_id=1, source_target_pairs={{0,192},{64,0},{128,64},{192,128},{1,193},{65,1},{129,65},{193,129... | collective-permute-start | bytes 1179656 | tf_op jit(solution)/shard_map/along_y/ppermute | solution.py:257
  88.7 26.0 %collective-permute-start.19 = (bf16[32,48,128]{2,1,0:T(8,128)(2,1)}, bf16[32,48,128]{2,1,0:T(8,128)(2,1)}, u32[]{:S(2)}, u32[]{:S(2)}) collective-permute-start(bf16[32,48,128]{2,1,0:T(8,128)(2,1)} %get-tuple-element.42), channel_id=1, source_target_pairs={{0,128},{64,192},{128,0},{192,64},{1,129},{65,193},{129,1},{193,65... | collective-permute-start | bytes 1179656 | tf_op jit(solution)/shard_map/along_y/ppermute | solution.py:257
  94.0 20.7 %collective-permute-start.20 = (bf16[32,48,128]{2,1,0:T(8,128)(2,1)}, bf16[32,48,128]{2,1,0:T(8,128)(2,1)}, u32[]{:S(2)}, u32[]{:S(2)}) collective-permute-start(bf16[32,48,128]{2,1,0:T(8,128)(2,1)} %get-tuple-element.43), channel_id=1, source_target_pairs={{0,64},{64,128},{128,192},{192,0},{1,65},{65,129},{129,193},{193,1... | collective-permute-start | bytes 1179656 | tf_op jit(solution)/shard_map/along_y/ppermute | solution.py:257
  102.4 24.0 %all-to-all-start = ((bf16[128,48,128]{2,1,0:T(8,128)(2,1)}), bf16[128,48,128]{2,1,0:T(8,128)(2,1)S(1)}, u32[]{:S(2)}, u32[]{:S(2)}) async-start(bf16[128,48,128]{2,1,0:T(8,128)(2,1)} %pick_x.7), calls=%async_computation | async-start | bytes 3145728 | tf_op jit(solution)/shard_map/along_x/all_to_all | solution.py:281
  110.5 0.8 copy-start.5
  111.3 27.2 %collective-permute-start.21 = (bf16[32,48,128]{2,1,0:T(8,128)(2,1)}, bf16[32,48,128]{2,1,0:T(8,128)(2,1)}, u32[]{:S(2)}, u32[]{:S(2)}) collective-permute-start(bf16[32,48,128]{2,1,0:T(8,128)(2,1)} %get-tuple-element.45), channel_id=1, source_target_pairs={{0,192},{64,0},{128,64},{192,128},{1,193},{65,1},{129,65},{193,129... | collective-permute-start | bytes 1179656 | tf_op jit(solution)/shard_map/along_y/ppermute | solution.py:257
  113.2 25.3 %collective-permute-start.22 = (bf16[32,48,128]{2,1,0:T(8,128)(2,1)}, bf16[32,48,128]{2,1,0:T(8,128)(2,1)}, u32[]{:S(2)}, u32[]{:S(2)}) collective-permute-start(bf16[32,48,128]{2,1,0:T(8,128)(2,1)} %get-tuple-element.46), channel_id=1, source_target_pairs={{0,128},{64,192},{128,0},{192,64},{1,129},{65,193},{129,1},{193,65... | collective-permute-start | bytes 1179656 | tf_op jit(solution)/shard_map/along_y/ppermute | solution.py:257
  114.7 23.8 %collective-permute-start.23 = (bf16[32,48,128]{2,1,0:T(8,128)(2,1)}, bf16[32,48,128]{2,1,0:T(8,128)(2,1)}, u32[]{:S(2)}, u32[]{:S(2)}) collective-permute-start(bf16[32,48,128]{2,1,0:T(8,128)(2,1)} %get-tuple-element.47), channel_id=1, source_target_pairs={{0,64},{64,128},{128,192},{192,0},{1,65},{65,129},{129,193},{193,1... | collective-permute-start | bytes 1179656 | tf_op jit(solution)/shard_map/along_y/ppermute | solution.py:257
  126.4 24.3 %all-to-all-start.3 = ((bf16[128,48,128]{2,1,0:T(8,128)(2,1)}), bf16[128,48,128]{2,1,0:T(8,128)(2,1)}, u32[]{:S(2)}, u32[]{:S(2)}) async-start(bf16[128,48,128]{2,1,0:T(8,128)(2,1)} %pick_x.9), calls=%async_computation.3 | async-start | bytes 3145728 | tf_op jit(solution)/shard_map/along_x/all_to_all | solution.py:281
  132.2 6.4 %copy-start.6 = (bf16[32,48,128]{2,1,0:T(8,128)(2,1)S(1)}, bf16[32,48,128]{2,1,0:T(8,128)(2,1)}, u32[]{:S(2)}) copy-start(bf16[32,48,128]{2,1,0:T(8,128)(2,1)} %copy-done.5) | copy-start | bytes 1179652
  135.5 0.8 copy-start.3
  136.3 24.3 %collective-permute-start.24 = (bf16[32,48,128]{2,1,0:T(8,128)(2,1)}, bf16[32,48,128]{2,1,0:T(8,128)(2,1)}, u32[]{:S(2)}, u32[]{:S(2)}) collective-permute-start(bf16[32,48,128]{2,1,0:T(8,128)(2,1)} %get-tuple-element.49), channel_id=1, source_target_pairs={{0,192},{64,0},{128,64},{192,128},{1,193},{65,1},{129,65},{193,129... | collective-permute-start | bytes 1179656 | tf_op jit(solution)/shard_map/along_y/ppermute | solution.py:257
  136.9 24.9 %collective-permute-start.25 = (bf16[32,48,128]{2,1,0:T(8,128)(2,1)}, bf16[32,48,128]{2,1,0:T(8,128)(2,1)}, u32[]{:S(2)}, u32[]{:S(2)}) collective-permute-start(bf16[32,48,128]{2,1,0:T(8,128)(2,1)} %get-tuple-element.50), channel_id=1, source_target_pairs={{0,128},{64,192},{128,0},{192,64},{1,129},{65,193},{129,1},{193,65... | collective-permute-start | bytes 1179656 | tf_op jit(solution)/shard_map/along_y/ppermute | solution.py:257
  138.5 23.4 %collective-permute-start.26 = (bf16[32,48,128]{2,1,0:T(8,128)(2,1)}, bf16[32,48,128]{2,1,0:T(8,128)(2,1)}, u32[]{:S(2)}, u32[]{:S(2)}) collective-permute-start(bf16[32,48,128]{2,1,0:T(8,128)(2,1)} %get-tuple-element.51), channel_id=1, source_target_pairs={{0,64},{64,128},{128,192},{192,0},{1,65},{65,129},{129,193},{193,1... | collective-permute-start | bytes 1179656 | tf_op jit(solution)/shard_map/along_y/ppermute | solution.py:257
  150.6 23.3 %all-to-all-start.4 = ((bf16[128,48,128]{2,1,0:T(8,128)(2,1)}), bf16[128,48,128]{2,1,0:T(8,128)(2,1)}, u32[]{:S(2)}, u32[]{:S(2)}) async-start(bf16[128,48,128]{2,1,0:T(8,128)(2,1)} %pick_x.10), calls=%async_computation.4 | async-start | bytes 3145728 | tf_op jit(solution)/shard_map/along_x/all_to_all | solution.py:281
  156.4 5.4 %copy-start.4 = (bf16[32,48,128]{2,1,0:T(8,128)(2,1)S(1)}, bf16[32,48,128]{2,1,0:T(8,128)(2,1)}, u32[]{:S(2)}) copy-start(bf16[32,48,128]{2,1,0:T(8,128)(2,1)} %copy-done.3) | copy-start | bytes 1179652
  159.7 20.8 %collective-permute-start.15 = (bf16[32,48,128]{2,1,0:T(8,128)(2,1)}, bf16[32,48,128]{2,1,0:T(8,128)(2,1)}, u32[]{:S(2)}, u32[]{:S(2)}) collective-permute-start(bf16[32,48,128]{2,1,0:T(8,128)(2,1)} %get-tuple-element.37), channel_id=1, source_target_pairs={{0,192},{64,0},{128,64},{192,128},{1,193},{65,1},{129,65},{193,129... | collective-permute-start | bytes 1179656 | tf_op jit(solution)/shard_map/along_y/ppermute | solution.py:257
  159.8 20.7 %collective-permute-start.16 = (bf16[32,48,128]{2,1,0:T(8,128)(2,1)}, bf16[32,48,128]{2,1,0:T(8,128)(2,1)}, u32[]{:S(2)}, u32[]{:S(2)}) collective-permute-start(bf16[32,48,128]{2,1,0:T(8,128)(2,1)} %get-tuple-element.38), channel_id=1, source_target_pairs={{0,128},{64,192},{128,0},{192,64},{1,129},{65,193},{129,1},{193,65... | collective-permute-start | bytes 1179656 | tf_op jit(solution)/shard_map/along_y/ppermute | solution.py:257
  160.6 19.9 %collective-permute-start.17 = (bf16[32,48,128]{2,1,0:T(8,128)(2,1)}, bf16[32,48,128]{2,1,0:T(8,128)(2,1)}, u32[]{:S(2)}, u32[]{:S(2)}) collective-permute-start(bf16[32,48,128]{2,1,0:T(8,128)(2,1)} %get-tuple-element.39), channel_id=1, source_target_pairs={{0,64},{64,128},{128,192},{192,0},{1,65},{65,129},{129,193},{193,1... | collective-permute-start | bytes 1179656 | tf_op jit(solution)/shard_map/along_y/ppermute | solution.py:257
  174.0 22.4 %all-to-all-start.5 = ((bf16[128,48,128]{2,1,0:T(8,128)(2,1)}), bf16[128,48,128]{2,1,0:T(8,128)(2,1)}, u32[]{:S(2)}, u32[]{:S(2)}) async-start(bf16[128,48,128]{2,1,0:T(8,128)(2,1)} %pick_x.11), calls=%async_computation.5 | async-start | bytes 3145728 | tf_op jit(solution)/shard_map/along_x/all_to_all | solution.py:281
  184.0 18.4 %copy-start.2 = (f32[32]{0:T(128)S(1)}, f32[32]{0:T(128)}, u32[]{:S(2)}) copy-start(f32[32]{0:T(128)} %fock.3) | copy-start | bytes 388
  196.4 21.5 %all-to-all-start.1 = ((bf16[128,48,128]{2,1,0:T(8,128)(2,1)}), bf16[128,48,128]{2,1,0:T(8,128)(2,1)}, u32[]{:S(2)}, u32[]{:S(2)}) async-start(bf16[128,48,128]{2,1,0:T(8,128)(2,1)} %pick_x.8), calls=%async_computation.1 | async-start | bytes 3145728 | tf_op jit(solution)/shard_map/along_x/all_to_all | solution.py:281
  230.2 5.1 %copy-start.11 = (f32[8,384]{1,0:T(8,128)S(1)}, f32[8,384]{1,0:T(8,128)}, u32[]{:S(2)}) copy-start(f32[8,384]{1,0:T(8,128)} %param.12) | copy-start | bytes 36868
  230.2 27.9 %all-to-all-start.6 = ((bf16[4,8,96,384]{3,2,1,0:T(8,128)(2,1)}), bf16[4,8,96,384]{3,2,1,0:T(8,128)(2,1)S(1)}, u32[]{:S(2)}, u32[]{:S(2)}) async-start(bf16[4,8,96,384]{3,2,1,0:T(8,128)(2,1)} %couple.3), calls=%async_computation.6 | async-start | bytes 4718592 | tf_op jit(solution)/shard_map/sum_x/all_to_all | solution.py:294
  235.3 23.1 %copy-start.7 = (bf16[8,96,384]{2,1,0:T(8,128)(2,1)S(1)}, bf16[8,96,384]{2,1,0:T(8,128)(2,1)}, u32[]{:S(2)}) copy-start(bf16[8,96,384]{2,1,0:T(8,128)(2,1)} %in_ref.3) | copy-start | bytes 1769476
  235.3 23.1 %copy-start.13 = (f32[8]{0:T(128)S(1)}, f32[8]{0:T(128)}, u32[]{:S(2)}) copy-start(f32[8]{0:T(128)} %param.13) | copy-start | bytes 100
  258.1 1.1 copy-start.10
  258.1 3.0 %copy-start.1 = (s32[8192]{0:T(1024)S(1)}, s32[8192]{0:T(1024)}, u32[]{:S(2)}) copy-start(s32[8192]{0:T(1024)} %param.15) | copy-start | bytes 98308
Sparse Core Ops, SparseCore 0:
  9.9 60.5 all-gather.2
